TPU v7x, 32 devices: a whole 2x2x4 slice. The times are simulated.
32 devices in a mesh: ax: 4 (over y, x), ay: 8 (over z, core).
Axes of the slice: x: 2, y: 2, z: 4, core: 2. Of those that a mesh axis runs over, the one named last changes fastest.
Arguments:
- noise: float32 [16, 1024, 2048], P(None, ('ax', 'ay')), may hold values from -6 to 6
- kappa: float32 [16, 1024, 2048], P(None, 'ax', 'ay'), may hold values from 0.05 to 2
- mask: int32 [1024, 2048], P('ax', 'ay'), may hold values 0 or 1
Outputs:
- sample: float32 [16, 1024, 2048], P(None, 'ax', 'ay')
All inputs are finite; a program needn't handle non-finite values. No bound on the sum of `mask` on one device may be relied on, other than what follows from the above.
Results may differ from a plain program's by a relative error of at most 0.00002.
Values sent between devices are 32-bit elements; how exact they have to be, the bound alone decides.
No kernel may reach another device: no remote copies, remote signals or barrier semaphores. Data moves between devices by JAX's collectives and lax.ppermute only.
A program may use at most 128 MiB of HBM per device.

v0:
```python
import jax
import jax.numpy as jnp
from jax import lax
from jax.sharding import PartitionSpec as P


def extended(cells, sides, width):
    for axis, dim in sides:
        count = lax.axis_size(axis)
        ends = count - 1
        head = lax.slice_in_dim(cells, 0, width, axis=dim)
        tail = lax.slice_in_dim(cells, cells.shape[dim] - width, cells.shape[dim], axis=dim)
        cells = jnp.concatenate(
            [
                lax.ppermute(tail, axis, [(i, (i + 1) % count) for i in range(ends)]),
                cells,
                lax.ppermute(head, axis, [((i + 1) % count, i) for i in range(ends)]),
            ],
            axis=dim,
        )
    return cells


def neighbours(padded):
    centre = padded[:, 1:-1, 1:-1]
    with_ends = jnp.pad(centre, ((1, 1), (0, 0), (0, 0)))
    total = padded[:, 2:, 1:-1] + padded[:, :-2, 1:-1]
    total = total + padded[:, 1:-1, 2:] + padded[:, 1:-1, :-2]
    return total + with_ends[2:] + with_ends[:-2]


def factors(kappa):
    pivots = []
    for layer_index in range(kappa.shape[0]):
        diagonal = 2.5 + kappa[layer_index]
        if layer_index > 0:
            diagonal = diagonal - pivots[-1]
        pivots.append(1.0 / diagonal)
    return pivots


def thomas(field, pivots):
    layers = field.shape[0]
    forward = []
    for layer_index in range(layers):
        current = field[layer_index]
        if layer_index > 0:
            current = current + forward[-1]
        forward.append(current * pivots[layer_index])
    result = [None] * layers
    solved = forward[layers - 1]
    result[layers - 1] = solved
    for layer_index in range(layers - 2, -1, -1):
        solved = forward[layer_index] + pivots[layer_index] * solved
        result[layer_index] = solved
    return jnp.stack(result, 0)


def body(noise, kappa, mask):
    layers = kappa.shape[0]
    stacked = jnp.concatenate([kappa, mask[None].astype(jnp.float32)], 0)
    strip_coef = lax.all_to_all(stacked, "ay", split_axis=1, concat_axis=2, tiled=True)
    strip_kappa = strip_coef[:layers]
    strip_mask = strip_coef[layers:]
    inverse = strip_mask / (6.0 + strip_kappa)
    pivots = factors(strip_kappa)
    field = inverse * noise
    for repeat in range(2):
        padded = extended(field, ((("ax", "ay"), 1),), 1)
        padded = jnp.pad(padded, ((0, 0), (0, 0), (1, 1)))
        field = inverse * (noise + neighbours(padded))
    strip_sample = thomas(field, pivots)
    return lax.all_to_all(strip_sample, "ay", split_axis=2, concat_axis=1, tiled=True)


def solution(mesh):
    in_specs = (P(None, ("ax", "ay"), None), P(None, "ax", "ay"), P("ax", "ay"))
    out_specs = P(None, "ax", "ay")
    return jax.shard_map(body, mesh=mesh, in_specs=in_specs, out_specs=out_specs, check_vma=False)
```

profile of v0, /device:TPU:0, one launch (start us, length us, event | category | flops | bytes accessed | tf_op | source)
XLA Modules:
  0.0 416.1 jit_solution(1570629278956678191)
XLA Ops:
  0.0 4.7 %copy.32 = f32[16,256,256]{2,0,1:T(8,128)S(1)} copy(f32[16,256,256]{2,1,0:T(8,128)} %param.4) | data formatting | bytes 8388608 | tf_op args[1]
  4.7 0.3 copy.33
  5.0 0.6 pad_maximum_fusion
  5.6 145.2 %all_to_all.33 = f32[17,256,256]{2,0,1:T(8,128)S(1)} all-to-all(f32[17,256,256]{2,0,1:T(8,128)S(1)} %pad_maximum_fusion), channel_id=1, replica_groups=mesh['ax'=4,'ay'=8] {'ay'}, dimensions={1} | all-to-all | bytes 8912896 | tf_op jit(solution)/shard_map/all_to_all | solution.py:62
  150.8 2.6 copy.51
  153.4 1.7 slice_add_fusion.31
  155.1 2.3 slice_add_fusion.4
  157.5 5.0 %add.1311 = f32[16,32,2048]{2,1,0:T(8,128)} reshape(f32[16,32,8,256]{3,2,1,0:T(8,128)} %slice_add_fusion.4) | data formatting | bytes 8388608 | tf_op jit(solution)/shard_map/add | solution.py:65
  162.5 4.3 %fusion.34 = f32[16,32,2048]{2,1,0:T(8,128)S(1)} fusion(f32[16,32,2048]{2,1,0:T(8,128)} %param.3, f32[16,32,2048]{2,1,0:T(8,128)} %add.1311, f32[32,2048]{1,0:T(8,128)S(1)} %bitcast.54), kind=kLoop, calls=%fused_computation.126 | loop fusion | flops 2097152 | bytes 12845056 | tf_op jit(solution)/shard_map/mul | solution.py:67
  166.8 0.2 fusion.44
  167.1 1.3 collective-permute-start
  168.4 3.2 collective-permute-start.1
  171.6 0.1 copy.36
  171.8 0.6 collective-permute-done.1
  172.6 4.4 %select_maximum_fusion.2 = f32[16,34,2050]{2,1,0:T(8,128)} fusion(f32[16,1,2048]{2,1,0:T(1,128)S(1)} %copy.36, f32[16,32,2048]{2,1,0:T(8,128)S(1)} %fusion.34, f32[16,1,2048]{2,1,0:T(1,128)S(1)} %copy.38), kind=kLoop, calls=%fused_computation.5 | loop fusion | flops 8921600 | bytes 8917248 | tf_op jit(solution)/shard_map/concatenate | solution.py:13
  177.0 7.5 %fusion.4 = f32[16,32,2048]{2,1,0:T(8,128)S(1)} fusion(f32[16,32,2048]{2,1,0:T(8,128)} %param.3, f32[16,32,2048]{2,1,0:T(8,128)S(1)} %fusion.34, f32[16,34,2050]{2,1,0:T(8,128)} %select_maximum_fusion.2, f32[16,1,2048]{2,1,0:T(1,128)S(1)} %copy.38, f32[16,1,2048]{2,1,0:T(1,128)S(1)} %copy.36, f32[16,32,2048]{2,1,0:T(8,128)S(1)} %copy-done, ...), kind=kLoop, calls=%fused_computation.16 | loop fusion | flops 10485760 | bytes 25690112 | tf_op jit(solution)/shard_map/mul | solution.py:71
  184.5 2.0 copy-done.2
  186.6 0.2 fusion.43
  186.8 1.4 collective-permute-start.2
  188.2 0.7 copy.43
  188.9 4.2 %collective-permute-start.3 = (f32[16,1,2048]{2,0,1:T(8,128)}, f32[16,1,2048]{2,0,1:T(8,128)S(1)}, u32[]{:S(2)}, u32[]{:S(2)}) collective-permute-start(f32[16,1,2048]{2,0,1:T(8,128)} %copy.43), channel_id=1, source_target_pairs={{0,1},{1,2},{2,3},{3,4},{4,5},{5,6},{6,7},{7,8},{8,9},{9,10},{10,1... | collective-permute-start | bytes 393224 | tf_op jit(solution)/shard_map/ppermute | solution.py:15
  193.1 1.0 add.1363
  194.1 1.7 add.1366
  195.8 1.7 add.1327
  197.5 1.7 add.1330
  199.2 1.7 add.1333
  200.9 1.7 add.1336
  202.6 0.7 add.1339
  203.4 0.7 add.1342
  204.1 0.8 add.1345
  204.9 0.8 add.1348
  205.6 0.8 add.1351
  206.4 0.8 add.1354
  207.2 0.7 add.1357
  207.9 0.7 add.1360
  208.6 0.8 add.1369
  209.4 0.8 div.777
  210.2 1.0 copy.42
  211.4 0.6 copy-done.5
  212.0 4.6 %select_maximum_fusion = f32[16,34,2050]{2,1,0:T(8,128)S(1)} fusion(f32[16,1,2048]{2,1,0:T(1,128)S(1)} %copy.42, f32[16,32,2048]{2,1,0:T(8,128)} %copy-done.2, f32[16,1,2048]{2,1,0:T(1,128)S(1)} %copy.44), kind=kLoop, calls=%fused_computation.3 | loop fusion | flops 8921600 | bytes 8917248 | tf_op jit(solution)/shard_map/concatenate | solution.py:13
  216.7 7.5 %fusion.8 = f32[16,32,2048]{2,1,0:T(8,128)} fusion(f32[16,32,2048]{2,1,0:T(8,128)} %param.3, f32[16,32,2048]{2,1,0:T(8,128)S(1)} %copy-done.3, f32[16,34,2050]{2,1,0:T(8,128)S(1)} %select_maximum_fusion, f32[16,1,2048]{2,1,0:T(1,128)} %copy-done.5, f32[16,1,2048]{2,1,0:T(1,128)S(1)} %copy.42, f32[16,32,2048]{2,1,0:T(8,128)S(1)} %copy-done.1, ...), kind=kLoop, calls=%fused_computation.20 | loop fusion | flops 10485760 | bytes 25690112 | tf_op jit(solution)/shard_map/mul | solution.py:71
  224.2 5.1 %add_dynamic-update-slice_fusion = (f32[16,32,2048]{2,1,0:T(8,128)}, f32[1,32,2048]{2,1,0:T(8,128)S(1)}, f32[1,32,2048]{2,1,0:T(8,128)S(1)}, f32[1,32,2048]{2,1,...) fusion(f32[1,32,2048]{2,1,0:T(8,128)} %div.777, ...), kind=kLoop, calls=%fused_computation.81 | loop fusion | flops 5963775 | bytes 14155776
  229.3 0.7 constant_dynamic-update-slice_fusion.7
  230.0 1.7 fusion.33
  231.7 0.7 constant_dynamic-update-slice_fusion.6
  232.5 1.7 fusion.32
  234.2 0.7 constant_dynamic-update-slice_fusion.5
  234.9 1.7 fusion.31
  236.6 0.7 constant_dynamic-update-slice_fusion.4
  237.4 1.7 fusion.30
  239.1 0.7 constant_dynamic-update-slice_fusion.3
  239.8 1.7 fusion.29
  241.6 0.7 constant_dynamic-update-slice_fusion.2
  242.3 1.7 fusion.28
  244.0 0.7 constant_dynamic-update-slice_fusion.1
  244.7 1.8 fusion.27
  246.5 0.7 constant_dynamic-update-slice_fusion
  247.2 12.5 %copy.47 = f32[16,32,2048]{1,0,2:T(8,128)} copy(f32[16,32,2048]{2,1,0:T(8,128)} %constant_dynamic-update-slice_fusion) | data formatting | bytes 8388608 | tf_op jit(solution)/shard_map/stack | solution.py:56
  259.7 12.8 %reshape.925 = f32[8,1,131072]{2,1,0:T(1,128)} reshape(f32[2048,16,32]{2,1,0:T(8,128)} %bitcast.49) | data formatting | bytes 8388608
  272.5 104.5 %all_to_all.34 = f32[8,1,131072]{2,1,0:T(1,128)} all-to-all(f32[8,1,131072]{2,1,0:T(1,128)} %reshape.925), channel_id=1, replica_groups=mesh['ax'=4,'ay'=8] {'ay'}, dimensions={0} | all-to-all | bytes 8388608 | tf_op jit(solution)/shard_map/all_to_all | solution.py:73
  377.1 0.5 broadcast.1589
  377.6 13.7 %reduce = f32[8,131072]{1,0:T(8,128)} reduce(f32[8,1,131072]{2,1,0:T(1,128)} %all_to_all.34, f32[]{:T(128)} %broadcast.1589), dimensions={1}, to_apply=%all_to_all.27.reduce_sub_computation | reduce | bytes 8388612 | tf_op jit(solution)/shard_map/all_to_all | solution.py:73
  391.3 13.4 %reshape.926 = f32[2048,16,32]{2,1,0:T(8,128)} reshape(f32[8,131072]{1,0:T(8,128)} %reduce) | data formatting | bytes 8388608
  404.7 11.4 %copy.48 = f32[16,8,32,256]{3,2,1,0:T(8,128)} copy(f32[16,8,32,256]{2,0,3,1:T(8,128)} %bitcast.50) | data formatting | bytes 8388608 | tf_op jit(solution)/shard_map/all_to_all | solution.py:73
  (34 shorter events, 0.7 us)
Async XLA Ops:
  0.0 4.7 %copy-start.12 = (s32[256,256]{1,0:T(8,128)S(1)}, s32[256,256]{1,0:T(8,128)}, u32[]{:S(2)}) copy-start(s32[256,256]{1,0:T(8,128)} %param.5) | copy-start | bytes 786436
  167.1 4.6 %collective-permute-start = (f32[16,1,2048]{2,0,1:T(8,128)S(1)}, f32[16,1,2048]{2,0,1:T(8,128)S(1)}, u32[]{:S(2)}, u32[]{:S(2)}) collective-permute-start(f32[16,1,2048]{2,0,1:T(8,128)S(1)} %copy.35), channel_id=1, source_target_pairs={{1,0},{2,1},{3,2},{4,3},{5,4},{6,5},{7,6},{8,7},{9,8},{10,9},{11,1... | collective-permute-start | bytes 393224 | tf_op jit(solution)/shard_map/ppermute | solution.py:17
  168.4 4.0 collective-permute-start.1
  172.6 4.5 %copy-start = (f32[16,32,2048]{2,1,0:T(8,128)S(1)}, f32[16,32,2048]{2,1,0:T(8,128)}, u32[]{:S(2)}) copy-start(f32[16,32,2048]{2,1,0:T(8,128)} %add.1311) | copy-start | bytes 12582916
  184.5 2.0 copy-start.2
  186.5 16.1 %copy-start.11 = (f32[1,32,8,256]{3,2,1,0:T(8,128)S(1)}, f32[1,32,8,256]{3,2,1,0:T(8,128)}, u32[]{:S(2)}) copy-start(f32[1,32,8,256]{3,2,1,0:T(8,128)} %get-tuple-element.38) | copy-start | bytes 786436
  186.5 16.8 %copy-start.10 = (f32[1,32,8,256]{3,2,1,0:T(8,128)S(1)}, f32[1,32,8,256]{3,2,1,0:T(8,128)}, u32[]{:S(2)}) copy-start(f32[1,32,8,256]{3,2,1,0:T(8,128)} %get-tuple-element.37) | copy-start | bytes 786436
  186.5 17.6 %copy-start.9 = (f32[1,32,8,256]{3,2,1,0:T(8,128)S(1)}, f32[1,32,8,256]{3,2,1,0:T(8,128)}, u32[]{:S(2)}) copy-start(f32[1,32,8,256]{3,2,1,0:T(8,128)} %get-tuple-element.36) | copy-start | bytes 786436
  186.5 18.3 %copy-start.8 = (f32[1,32,8,256]{3,2,1,0:T(8,128)S(1)}, f32[1,32,8,256]{3,2,1,0:T(8,128)}, u32[]{:S(2)}) copy-start(f32[1,32,8,256]{3,2,1,0:T(8,128)} %get-tuple-element.35) | copy-start | bytes 786436
  186.5 19.1 %copy-start.7 = (f32[1,32,8,256]{3,2,1,0:T(8,128)S(1)}, f32[1,32,8,256]{3,2,1,0:T(8,128)}, u32[]{:S(2)}) copy-start(f32[1,32,8,256]{3,2,1,0:T(8,128)} %get-tuple-element.34) | copy-start | bytes 786436
  186.6 19.8 %copy-start.6 = (f32[1,32,8,256]{3,2,1,0:T(8,128)S(1)}, f32[1,32,8,256]{3,2,1,0:T(8,128)}, u32[]{:S(2)}) copy-start(f32[1,32,8,256]{3,2,1,0:T(8,128)} %get-tuple-element.33) | copy-start | bytes 786436
  186.8 23.4 %collective-permute-start.2 = (f32[16,1,2048]{2,0,1:T(8,128)S(1)}, f32[16,1,2048]{2,0,1:T(8,128)}, u32[]{:S(2)}, u32[]{:S(2)}) collective-permute-start(f32[16,1,2048]{2,0,1:T(8,128)S(1)} %copy.41), channel_id=1, source_target_pairs={{1,0},{2,1},{3,2},{4,3},{5,4},{6,5},{7,6},{8,7},{9,8},{10,9},{11,1... | collective-permute-start | bytes 393224 | tf_op jit(solution)/shard_map/ppermute | solution.py:17
  188.9 22.3 %collective-permute-start.3 = (f32[16,1,2048]{2,0,1:T(8,128)}, f32[16,1,2048]{2,0,1:T(8,128)S(1)}, u32[]{:S(2)}, u32[]{:S(2)}) collective-permute-start(f32[16,1,2048]{2,0,1:T(8,128)} %copy.43), channel_id=1, source_target_pairs={{0,1},{1,2},{2,3},{3,4},{4,5},{5,6},{6,7},{7,8},{8,9},{9,10},{10,1... | collective-permute-start | bytes 393224 | tf_op jit(solution)/shard_map/ppermute | solution.py:15
  211.4 0.6 copy-start.5
  212.0 4.6 %copy-start.1 = (f32[16,32,2048]{2,1,0:T(8,128)S(1)}, f32[16,32,2048]{2,1,0:T(8,128)}, u32[]{:S(2)}) copy-start(f32[16,32,2048]{2,1,0:T(8,128)} %add.1311) | copy-start | bytes 12582916
  212.0 4.7 %copy-start.3 = (f32[16,32,2048]{2,1,0:T(8,128)S(1)}, f32[16,32,2048]{2,1,0:T(8,128)}, u32[]{:S(2)}) copy-start(f32[16,32,2048]{2,1,0:T(8,128)} %copy-done.2) | copy-start | bytes 12582916
  234.2 10.5 %copy-start.4 = (f32[1,32,2048]{2,1,0:T(8,128)S(1)}, f32[1,32,2048]{2,1,0:T(8,128)}, u32[]{:S(2)}) copy-start(f32[1,32,2048]{2,1,0:T(8,128)} %add.1366) | copy-start | bytes 786436
where the time goes:
time: 418 us; the launch traced here: 416 us
  blocking collectives  250 us (60%)
  local copies, waits for them, and re-layouts  91.4 us (22%)
  other arithmetic  63.9 us (15%)
  starting transfers between devices  10.1 us (2%)
    all_to_all x1, blocking collectives, body(): lax.all_to_all(stacked, 'ay', split_axis=1, concat_axis=2, tiled=True)  145 us
    all_to_all x1, blocking collectives, body(): lax.all_to_all(strip_sample, 'ay', split_axis=2, concat_axis=1, tiled=True)  105 us
    unnamed x37, local copies, waits for them, and re-layouts  38.8 us
    unnamed x8, other arithmetic  17.2 us
    add x15, local copies, waits for them, and re-layouts, factors(): diagonal = 2.5 + kappa[layer_index]  16.2 us
    mul x2, other arithmetic, body(): field = inverse * (noise + neighbours(padded))  15 us
    all_to_all x1, other arithmetic, body(): lax.all_to_all(strip_sample, 'ay', split_axis=2, concat_axis=1, tiled=True)  13.7 us
    another operation x2, local copies, waits for them, and re-layouts, thomas(): return jnp.stack(result, 0)  13.2 us
  transfers between devices with their start and end apart: 4, of which 1 were waited for; matrix products, arithmetic and copies ran while one was open for 5% of the time, Pallas kernels for 0%

commit v1 on v0

v1 whole, which is shorter than its diff:
```python
import functools

import jax
import jax.numpy as jnp
from jax import lax
from jax.experimental import pallas as pl
from jax.experimental.pallas import tpu as pltpu
from jax.sharding import PartitionSpec as P

LANES = 128
SLOT = 8
GROUP = 8


def lanes_of(rows):
    return lax.broadcasted_iota(jnp.int32, (rows, LANES), 1)


def pack_kernel(cells, out):
    layers, rows, columns = cells.shape
    lane = lanes_of(rows)

    def step(layer, packed):
        both = jnp.where(lane < LANES // 2, cells[layer, :, :LANES], cells[layer, :, columns - LANES :])
        return jnp.where(lane // SLOT == layer, pltpu.roll(both, layer * SLOT + 4, 1), packed)

    out[...] = lax.fori_loop(0, layers, step, jnp.zeros((rows, LANES), jnp.float32))


def pack(cells, columns, rows):
    layers, height, width = cells.shape
    return pl.pallas_call(
        pack_kernel,
        grid=(width // columns, height // rows),
        in_specs=[pl.BlockSpec((layers, rows, columns), lambda b, r: (0, r, b))],
        out_specs=pl.BlockSpec((None, rows, LANES), lambda b, r: (b, r, 0)),
        out_shape=jax.ShapeDtypeStruct((width // columns, height, LANES), jnp.float32),
    )(cells)


def around(cells, sides, layer, first, rows):
    tiles = cells.shape[1]
    lane = lanes_of(rows)
    side = pltpu.roll(sides, LANES - 3 - layer * SLOT, 1)
    centre = [cells[layer + 1, t, pl.ds(first, rows), :] for t in range(tiles)]
    left = [pltpu.roll(x, 1, 1) for x in centre]
    right = [pltpu.roll(x, LANES - 1, 1) for x in centre]
    totals = []
    for t in range(tiles):
        total = cells[layer + 1, t, pl.ds(first + 1, rows), :] + cells[layer + 1, t, pl.ds(first - 1, rows), :]
        total = total + jnp.where(lane == 0, side if t == 0 else left[t - 1], left[t])
        total = total + jnp.where(lane == LANES - 1, side if t == tiles - 1 else right[t + 1], right[t])
        totals.append(total + cells[layer, t, pl.ds(first, rows), :] + cells[layer + 2, t, pl.ds(first, rows), :])
    return totals


def window_kernel(half, is_far, *refs):
    if is_far:
        inverse_in, pivots_in, packed_noise, packed_inverse, near, end, *pieces = refs[: 6 + half]
        rest = refs[7 + half :]
    else:
        inverse_in, pivots_in, packed_noise, packed_inverse, near = refs[:5]
        rest = refs[5:]
    out, noise, inverse, pivots, initial, middle, forward, result, sems, out_sems = rest
    layers, groups, _, columns = pivots.shape
    tiles = columns // LANES
    span = groups + 2
    rows, kept = span * GROUP, groups * GROUP
    me = lax.axis_index("ay")
    upper = me // half
    if is_far:
        start = (groups - 2) * (1 - upper)
        depth = pieces[0].shape[1]
        copies = [
            pltpu.make_async_copy(near, noise.at[:, pl.ds((span - 2) * upper, 2)], sems.at[2]),
            pltpu.make_async_copy(end, noise.at[:, pl.ds((span - 1) * (1 - upper), 1)], sems.at[3]),
        ]
        for i, piece in enumerate(pieces):
            place = 2 - upper + depth * ((me % half) ^ (half - 1 - i))
            copies.append(pltpu.make_async_copy(piece, noise.at[:, pl.ds(place, depth)], sems.at[4 + i]))
    else:
        start = (groups + 2) * upper
        copies = [pltpu.make_async_copy(near, noise, sems.at[2])]
    copies.append(pltpu.make_async_copy(inverse_in.at[:, pl.ds(start, span)], inverse, sems.at[0]))
    pivot_copy = pltpu.make_async_copy(pivots_in.at[:, pl.ds(start, groups)], pivots, sems.at[1])
    for copy in copies:
        copy.start()
    pivot_copy.start()

    for cells in (initial, middle):
        cells[0] = jnp.zeros(cells.shape[1:], jnp.float32)
        cells[layers + 1] = jnp.zeros(cells.shape[1:], jnp.float32)
    forward[0] = jnp.zeros(forward.shape[1:], jnp.float32)
    result[layers] = jnp.zeros(result.shape[1:], jnp.float32)
    lane = lanes_of(rows)
    place = lane % SLOT
    side_noise = packed_noise[pl.ds(start, span)].reshape(rows, LANES)
    side_inverse = packed_inverse[pl.ds(start, span)].reshape(rows, LANES)
    for copy in copies:
        copy.wait()

    def first_step(layer, own):
        field = (inverse[layer] * noise[layer]).reshape(rows, columns)
        for t in range(tiles):
            initial[layer + 1, t, pl.ds(GROUP, rows), :] = field[:, t * LANES : (t + 1) * LANES]
        both = jnp.where(lane == LANES - 1, field[:, columns - LANES :], field[:, :LANES])
        return jnp.where(lane // SLOT == layer, pltpu.roll(both, layer * SLOT + 1, 1), own)

    own = lax.fori_loop(0, layers, first_step, jnp.zeros((rows, LANES), jnp.float32))

    side = jnp.where(place < 2, own, side_inverse * side_noise)
    total = jnp.where(lane >= SLOT, pltpu.roll(side, SLOT, 1), 0.0)
    total = total + jnp.where(lane < LANES - SLOT, pltpu.roll(side, LANES - SLOT, 1), 0.0)
    total = total + pltpu.roll(side, 1, 0) + pltpu.roll(side, rows - 1, 0)
    total = total + jnp.where(
        place == 3,
        pltpu.roll(side, 1, 1) + pltpu.roll(side, 2, 1),
        pltpu.roll(side, LANES - 1, 1) + pltpu.roll(side, 4, 1),
    )
    side_middle = side_inverse * (side_noise + total)
    side = jnp.where(place == 2, pltpu.roll(side, LANES - 2, 1), side)
    side_middle = jnp.where(place == 2, pltpu.roll(side_middle, LANES - 2, 1), side_middle)[GROUP : GROUP + kept]

    def second_step(layer, carry):
        totals = around(initial, side, layer, GROUP, rows)
        for t in range(tiles):
            part = pl.ds(t * LANES, LANES)
            field = inverse[layer, :, :, part] * (noise[layer, :, :, part] + totals[t].reshape(span, GROUP, LANES))
            middle[layer + 1, t, pl.ds(GROUP, rows), :] = field.reshape(rows, LANES)
        return carry

    lax.fori_loop(0, layers, second_step, 0)
    pivot_copy.wait()

    def third_step(layer, carry):
        totals = around(middle, side_middle, layer, 2 * GROUP, kept)
        inner = pl.ds(1, groups)
        for t in range(tiles):
            part = pl.ds(t * LANES, LANES)
            field = inverse[layer, inner, :, part] * (noise[layer, inner, :, part] + totals[t].reshape(groups, GROUP, LANES))
            forward[layer + 1, :, :, part] = (field + forward[layer, :, :, part]) * pivots[layer, :, :, part]
        return carry

    lax.fori_loop(0, layers, third_step, 0)

    def place_out(layer):
        return pltpu.make_async_copy(result.at[layer], out.at[layer, pl.ds(start, groups)], out_sems.at[layer])

    def last_step(step, carry):
        layer = layers - 1 - step
        result[layer] = forward[layer + 1] + pivots[layer] * result[layer + 1]
        place_out(layer).start()
        return carry

    lax.fori_loop(0, layers, last_step, 0)
    for layer in range(layers):
        place_out(layer).wait()


def window(inverse, pivots, packed_noise, packed_inverse, near, half, rest=(), partial=None):
    layers, total_groups, _, columns = pivots.shape
    is_far = partial is not None
    groups = total_groups // 2 + (1 if is_far else -1)
    span = groups + 2
    tiles = columns // LANES
    anywhere = pl.BlockSpec(memory_space=pl.ANY)
    whole = pl.BlockSpec(memory_space=pltpu.VMEM)
    operands = [inverse, pivots, packed_noise, packed_inverse, near, *rest]
    specs = [anywhere, anywhere, whole, whole, anywhere] + [anywhere] * len(rest)
    aliases = {}
    if is_far:
        aliases = {len(operands): 0}
        operands.append(partial)
        specs.append(anywhere)
    block = functools.partial(pltpu.VMEM, dtype=jnp.float32)
    padded = (layers + 2, tiles, (span + 2) * GROUP, LANES)
    return pl.pallas_call(
        functools.partial(window_kernel, half, is_far),
        in_specs=specs,
        out_specs=anywhere,
        out_shape=jax.ShapeDtypeStruct((layers, total_groups, GROUP, columns), jnp.float32),
        scratch_shapes=[
            block((layers, span, GROUP, columns)),
            block((layers, span, GROUP, columns)),
            block((layers, groups, GROUP, columns)),
            block(padded),
            block(padded),
            block((layers + 1, groups, GROUP, columns)),
            block((layers + 1, groups, GROUP, columns)),
            pltpu.SemaphoreType.DMA((4 + half,)),
            pltpu.SemaphoreType.DMA((layers,)),
        ],
        input_output_aliases=aliases,
        compiler_params=pltpu.CompilerParams(vmem_limit_bytes=32 * 1024 * 1024),
        cost_estimate=pl.CostEstimate(flops=20 * layers * kept_cells(groups, columns), bytes_accessed=16 * layers * kept_cells(groups, columns), transcendentals=0),
    )(*operands)


def kept_cells(groups, columns):
    return groups * GROUP * columns


def factors(kappa):
    pivots = []
    for layer_index in range(kappa.shape[0]):
        diagonal = 2.5 + kappa[layer_index]
        if layer_index > 0:
            diagonal = diagonal - pivots[-1]
        pivots.append(1.0 / diagonal)
    return jnp.stack(pivots, 0)


def columns_of(cells, owner, columns):
    return lax.dynamic_slice_in_dim(cells, owner * columns, columns, axis=2)


def rows_message(pairs_of_rows, corner):
    layers, two, columns = pairs_of_rows.shape
    flat = pairs_of_rows.reshape(layers * two, columns)
    corner = jnp.pad(corner, ((0, GROUP - 1), (0, columns - LANES)))
    return jnp.concatenate([flat, corner], 0)


def read_rows(message, layers, above):
    columns = message.shape[1]
    pair = message[: 2 * layers].reshape(layers, 2, columns)
    corner = message[2 * layers : 2 * layers + 1, :LANES]
    if above:
        return jnp.pad(pair, ((0, 0), (GROUP - 2, 0), (0, 0))), jnp.pad(corner, ((GROUP - 1, 0), (0, 0)))
    return jnp.pad(pair, ((0, 0), (0, GROUP - 2), (0, 0))), jnp.pad(corner, ((0, GROUP - 1), (0, 0)))


def fold(packed, columns):
    rows = packed.shape[-2]
    both = packed * four_lanes()
    both = both[..., : rows // 2, :] + jnp.roll(both[..., rows // 2 :, :], 4, axis=-1)
    wide = columns // LANES
    count = rows // 2 // GROUP
    parts = [both[..., i * GROUP : (i + 1) * GROUP, :] for i in range(count)]
    while len(parts) % wide:
        parts.append(jnp.zeros_like(parts[0]))
    lines = [jnp.concatenate(parts[i : i + wide], -1) for i in range(0, len(parts), wide)]
    return jnp.concatenate(lines, -2)


def unfold(message, rows):
    wide = message.shape[-1] // LANES
    lines = []
    for i in range(rows // 2 // GROUP):
        line, part = divmod(i, wide)
        lines.append(message[line * GROUP : (line + 1) * GROUP, part * LANES : (part + 1) * LANES])
    both = jnp.concatenate(lines, 0)
    return jnp.concatenate([both, jnp.roll(both, -4, axis=-1)], 0)


def four_lanes():
    place = jnp.arange(LANES) % SLOT
    return ((place >= 2) & (place < 6)).astype(jnp.float32)


def body(noise, kappa, mask):
    layers, rows, width = noise.shape
    count = lax.axis_size("ay")
    across = lax.axis_size("ax")
    half = count // 2
    columns = width // count
    height = rows * count
    depth = rows // GROUP
    me = lax.axis_index("ay")
    upper = me // half
    left_two = jnp.arange(LANES) % SLOT < 4

    def swap(cells, step):
        return lax.ppermute(cells, "ay", [(i, i ^ step) for i in range(count)])

    far = []
    token = me
    for step in range(count - 1, half - 1, -1):
        piece = columns_of(noise, token ^ step, columns)
        piece, token = lax.optimization_barrier((piece, token))
        far.append(swap(piece, step).reshape(layers, depth, GROUP, columns))

    inverse = mask[None].astype(jnp.float32) / (6.0 + kappa)
    packed = pack(inverse, columns, rows)[0]
    from_left = lax.ppermute(packed, "ay", [(i, i + 1) for i in range(count - 1)])
    from_right = lax.ppermute(packed, "ay", [(i + 1, i) for i in range(count - 1)])
    sides = jnp.where(left_two, from_left, from_right)
    down = rows_message(inverse[:, -2:], sides[-1:])
    up = rows_message(inverse[:, :2], sides[:1])
    from_above = lax.ppermute(down, "ax", [(i, i + 1) for i in range(across - 1)])
    from_below = lax.ppermute(up, "ax", [(i + 1, i) for i in range(across - 1)])
    above, corner_above = read_rows(from_above, layers, True)
    below, corner_below = read_rows(from_below, layers, False)
    inverse = jnp.concatenate([above, inverse, below], 1).reshape(layers, -1, GROUP, columns)
    packed_inverse = jnp.concatenate([corner_above, sides, corner_below], 0).reshape(-1, GROUP, LANES)
    pivots = factors(kappa).reshape(layers, -1, GROUP, columns)

    blocks = pack(noise, columns, rows)
    nothing = jnp.zeros_like(blocks[:1])
    sides = jnp.where(left_two, jnp.concatenate([nothing, blocks[:-1]]), jnp.concatenate([blocks[1:], nothing]))
    folded = fold(sides, columns)

    outer = lax.dynamic_slice_in_dim(noise, jnp.where(me == 0, 0, rows - 2), 2, axis=1)
    corner = lax.dynamic_slice_in_dim(sides, jnp.where(me == 0, 0, rows - 1), 1, axis=1)
    messages = jnp.stack([rows_message(outer[:, :, d * columns : (d + 1) * columns], corner[d]) for d in range(count)])
    pairs_same, pairs_other = [], []
    last = count - 1
    for i in range(across - 1):
        pairs_same += [(i * count + last, (i + 1) * count + last), ((i + 1) * count, i * count)]
        pairs_other += [(i * count + last, (i + 1) * count + half - 1), ((i + 1) * count, i * count + half)]
    own_half = lax.dynamic_slice_in_dim(messages, upper * half, half, axis=0)
    other_half = lax.dynamic_slice_in_dim(messages, (1 - upper) * half, half, axis=0)
    ends = lax.ppermute(own_half, ("ax", "ay"), pairs_same) + lax.ppermute(other_half, ("ax", "ay"), pairs_other)

    relayed = swap(lax.dynamic_slice_in_dim(folded, (1 - upper) * half, half, axis=0), half)
    direct = lax.dynamic_slice_in_dim(folded, upper * half, half, axis=0)
    extras = jnp.concatenate([direct, relayed, ends], 1)
    lines = folded.shape[1]

    near_block = jnp.zeros((layers, height // 2 + GROUP, columns), jnp.float32)
    packed_noise = jnp.zeros((height + 2 * GROUP, LANES), jnp.float32)
    extra_of = []
    for step in range(half):
        partner = me ^ step
        piece = columns_of(noise, partner, columns)
        extra = lax.dynamic_index_in_dim(extras, partner % half, 0, keepdims=False)
        if step:
            message = jnp.concatenate([piece.reshape(layers * rows, columns), extra], 0)
            message = swap(message, step)
            piece, extra = message[: layers * rows].reshape(layers, rows, columns), message[layers * rows :]
        at = (partner % half) * rows + GROUP * (1 - upper)
        near_block = lax.dynamic_update_slice_in_dim(near_block, piece, at, axis=1)
        packed_noise = lax.dynamic_update_slice_in_dim(packed_noise, unfold(extra[:lines], rows), GROUP + partner * rows, axis=0)
        packed_noise = lax.dynamic_update_slice_in_dim(
            packed_noise, unfold(extra[lines : 2 * lines], rows), GROUP + (partner ^ half) * rows, axis=0
        )
        extra_of.append(extra[2 * lines :])
    extra_of = jnp.stack(extra_of)
    top = lax.dynamic_index_in_dim(extra_of, (me % half) ^ (half - 1), 0, keepdims=False)
    bottom = lax.dynamic_index_in_dim(extra_of, me % half, 0, keepdims=False)
    above, corner_above = read_rows(top, layers, True)
    below, corner_below = read_rows(bottom, layers, False)
    packed_noise = lax.dynamic_update_slice_in_dim(packed_noise, corner_above, 0, axis=0)
    packed_noise = lax.dynamic_update_slice_in_dim(packed_noise, corner_below, GROUP + height, axis=0)
    packed_noise = packed_noise.reshape(-1, GROUP, LANES)
    near_block = lax.dynamic_update_slice_in_dim(near_block, jnp.where(upper == 0, above, below), upper * (height // 2), axis=1)
    near_block = near_block.reshape(layers, -1, GROUP, columns)
    inner = lax.dynamic_slice_in_dim(near_block, (1 - upper) * (near_block.shape[1] - 2), 2, axis=1)
    end = jnp.where(upper == 0, below, above).reshape(layers, 1, GROUP, columns)

    partial = window(inverse, pivots, packed_noise, packed_inverse, near_block, half)
    sample = window(inverse, pivots, packed_noise, packed_inverse, inner, half, (end, *far), partial)
    return sample.reshape(layers, height, columns)


def solution(mesh):
    in_specs = (P(None, ("ax", "ay"), None), P(None, "ax", "ay"), P("ax", "ay"))
    out_specs = P(None, "ax", "ay")
    return jax.shard_map(body, mesh=mesh, in_specs=in_specs, out_specs=out_specs, check_vma=False)
```

time: 418 us -> 184 us (0.44)
  blocking collectives: 250 us -> 0 us
  local copies, waits for them, and re-layouts: 91.4 us -> 29.7 us
  Pallas kernels: 0 us -> 42.7 us
  waiting for transfers between devices: 0.63 us -> 38.5 us
  other arithmetic: 63.9 us -> 42.2 us
  starting transfers between devices: 10.1 us -> 28.4 us
    all_to_all x2 -> x0, blocking collectives: 250 us -> none  [the longest x1 145 us: body(): lax.all_to_all(stacked, 'ay', split_axis=1, concat_axis=2, tiled=True)]
    pallas_call x0 -> x4, Pallas kernels: none -> 42.7 us  [the longest x2 22.1 us: pack(): pl.pallas_call(pack_kernel, grid=(width // columns, height // rows), in_s...]
    ppermute x4 -> x14, waiting for transfers between devices: 0.63 us -> 38.5 us  [the longest x8 38.5 us: swap(): return lax.ppermute(cells, 'ay', [(i, i ^ step) for i in range(count)])]
    unnamed x37 -> x12, local copies, waits for them, and re-layouts: 38.8 us -> 2.2 us
    add x16 -> x0, local copies, waits for them, and re-layouts: 21.2 us -> none  [the longest x15 16.2 us: factors(): diagonal = 2.5 + kappa[layer_index]]
    mul x3 -> x1, other arithmetic: 19.3 us -> 0.02 us  [fold(): both = packed * four_lanes()]
    ppermute x4 -> x14, starting transfers between devices: 10.1 us -> 28.4 us  [the longest x8 14.4 us: swap(): return lax.ppermute(cells, 'ay', [(i, i ^ step) for i in range(count)])]
    all_to_all x3 -> x0, local copies, waits for them, and re-layouts: 14.5 us -> none  [the longest x2 11.9 us: body(): lax.all_to_all(strip_sample, 'ay', split_axis=2, concat_axis=1, tiled=True)]
  transfers between devices with their start and end apart: 4 -> 14, of which waited for: 1 -> 2; matrix products, arithmetic and copies ran while one was open for 5% -> 35% of each run, Pallas kernels for 0% -> 11%
where the time goes in v1:
time: 184 us; the launch traced here: 182 us
  Pallas kernels  42.7 us (23%)
  other arithmetic  42.2 us (23%)
  waiting for transfers between devices  38.5 us (21%)
  local copies, waits for them, and re-layouts  29.7 us (16%)
  starting transfers between devices  28.4 us (15%)
    ppermute x8, waiting for transfers between devices, swap(): return lax.ppermute(cells, 'ay', [(i, i ^ step) for i in range(count)])  38.5 us
    pallas_call x2, Pallas kernels, pack(): pl.pallas_call(pack_kernel, grid=(width // columns, height // rows), in_s...  22.1 us
    pallas_call x2, Pallas kernels, window(): pl.pallas_call(functools.partial(window_kernel, half, is_far), in_specs=s...  20.6 us
    unnamed x22, other arithmetic  18 us
    ppermute x8, starting transfers between devices, swap(): return lax.ppermute(cells, 'ay', [(i, i ^ step) for i in range(count)])  14.4 us
    dynamic_slice x4, local copies, waits for them, and re-layouts, columns_of(): return lax.dynamic_slice_in_dim(cells, owner * columns, columns, axis=2)  8.87 us
    concatenate x3, other arithmetic, body(): message = jnp.concatenate([piece.reshape(layers * rows, columns), extra], 0)  5.7 us
    ppermute x1, starting transfers between devices, body(): lax.ppermute(down, 'ax', [(i, i + 1) for i in range(across - 1)])  5.16 us
  transfers between devices with their start and end apart: 14, of which 2 were waited for; matrix products, arithmetic and copies ran while one was open for 35% of the time, Pallas kernels for 11%

profile of v1, /device:TPU:0, one launch (start us, length us, event | category | flops | bytes accessed | tf_op | source)
XLA Modules:
  0.0 182.1 jit_solution(3861903517298681520)
XLA Ops:
  0.0 1.0 convert_element_type.34
  1.0 4.8 %add_divide_fusion.cells = f32[16,256,256]{2,1,0:T(8,128)} fusion(f32[16,256,256]{2,1,0:T(8,128)} %param.4, f32[256,256]{1,0:T(8,128)S(1)} %convert_element_type.34), kind=kLoop, calls=%fused_computation.5 | loop fusion | flops 2097152 | bytes 8650752 | tf_op jit(solution)/shard_map/div | solution.py:283
  5.7 11.1 %shard_map.37 = f32[1,256,128]{2,1,0:T(8,128)} custom-call(f32[16,256,256]{2,1,0:T(8,128)} %add_divide_fusion.cells), custom_call_target="tpu_custom_call" | custom-call | tf_op jit(solution)/shard_map/pallas_call | solution.py:32
  16.8 1.3 collective-permute-start.1
  18.1 3.7 %collective-permute-start = (f32[256,128]{1,0:T(8,128)}, f32[256,128]{1,0:T(8,128)}, u32[]{:S(2)}, u32[]{:S(2)}) collective-permute-start(f32[256,128]{1,0:T(8,128)} %bitcast.133), channel_id=1, source_target_pairs={{0,1},{1,2},{2,3},{3,4},{4,5},{5,6},{6,7},{8,9},{9,10},{10,11},{11... | collective-permute-start | bytes 393224 | tf_op jit(solution)/shard_map/ppermute | solution.py:285
  21.8 11.0 %shard_map.38 = f32[8,32,128]{2,1,0:T(8,128)} custom-call(f32[16,32,2048]{2,1,0:T(8,128)} %cells.1), custom_call_target="tpu_custom_call" | custom-call | tf_op jit(solution)/shard_map/pallas_call | solution.py:32
  32.8 1.0 fusion.52
  34.7 3.4 %collective-permute-start.4 = (f32[4,8,256]{2,1,0:T(8,128)}, f32[4,8,256]{2,1,0:T(8,128)}, u32[]{:S(2)}, u32[]{:S(2)}) collective-permute-start(f32[4,8,256]{2,1,0:T(8,128)} %get-tuple-element.86), channel_id=1, source_target_pairs={{0,4},{1,5},{2,6},{3,7},{4,0},{5,1},{6,2},{7,3},{8,12},{9,13},{10,... | collective-permute-start | bytes 98312 | tf_op jit(solution)/shard_map/ppermute | solution.py:274
  38.1 1.6 constant_dynamic-slice_fusion.29
  40.1 0.7 constant_dynamic-slice_fusion.26
  40.8 1.3 collective-permute-start.6
  42.1 1.3 collective-permute-start.5
  43.6 1.9 %constant_dynamic-slice_fusion.19 = f32[16,32,256]{2,1,0:T(8,128)} fusion(f32[16,32,2048]{2,1,0:T(8,128)} %cells.1, s32[]{:T(128)S(6)} %select_n.210), kind=kLoop, calls=%fused_computation.148 | loop fusion | bytes 1048580 | tf_op jit(solution)/shard_map/dynamic_slice | solution.py:214
  45.5 1.9 %constant_dynamic-slice_fusion.18 = f32[16,32,256]{2,1,0:T(8,128)} fusion(f32[16,32,2048]{2,1,0:T(8,128)} %cells.1, s32[]{:T(128)S(6)} %select_n.211), kind=kLoop, calls=%fused_computation.147 | loop fusion | bytes 1048580 | tf_op jit(solution)/shard_map/dynamic_slice | solution.py:214
  47.4 1.9 %constant_dynamic-slice_fusion.17 = f32[16,32,256]{2,1,0:T(8,128)} fusion(f32[16,32,2048]{2,1,0:T(8,128)} %cells.1, s32[]{:T(128)S(6)} %select_n.212), kind=kLoop, calls=%fused_computation.146 | loop fusion | bytes 1048580 | tf_op jit(solution)/shard_map/dynamic_slice | solution.py:214
  49.3 1.0 fusion.48
  50.3 1.7 bitcast_dynamic-update-slice_fusion.15
  52.1 3.1 %constant_dynamic-slice_fusion.16 = (f32[16,32,256]{2,1,0:T(8,128)}, f32[16,136,256]{2,1,0:T(8,128)S(1)}, f32[16,32,256]{2,1,0:T(8,128)}, f32[16,32,256]{2,1,0:T(8,128)}, f32[16,32,256]{2,1,0:T(8,128)}) fusion(f32[16,32,2048]{2,1,0:T(8,128)} %cells.1, s32[]{:T(128)S(6)} %select_n.213, f32[16,136,256]{2,1,0:T(8,128)S(1)} %broadcast_in_dim.20, ...), kind=kLoop, calls=%fused_computation.145 | loop fusion | bytes 5242904 | tf_op jit(solution)/shard_map/dynamic_slice | solution.py:214
  55.4 2.0 %bitcast_dynamic-update-slice_fusion.14 = f32[16,32,8,256]{3,2,1,0:T(8,128)} fusion(f32[16,32,8,256]{3,2,1,0:T(8,128)} %bitcast_dynamic-update-slice_fusion.15, f32[16,256,256]{2,1,0:T(8,128)} %param.4), kind=kLoop, calls=%fused_computation.24 | loop fusion | flops 327680 | bytes 786432
  57.3 1.9 %bitcast_dynamic-update-slice_fusion.13 = f32[16,32,8,256]{3,2,1,0:T(8,128)} fusion(f32[16,32,8,256]{3,2,1,0:T(8,128)} %bitcast_dynamic-update-slice_fusion.14, f32[16,256,256]{2,1,0:T(8,128)} %param.4), kind=kLoop, calls=%fused_computation.23 | loop fusion | flops 524288 | bytes 1048576
  59.3 2.1 %bitcast_dynamic-update-slice_fusion.12 = (f32[16,32,8,256]{3,2,1,0:T(8,128)}, f32[1,256,256]{2,1,0:T(8,128)S(1)}) fusion(f32[16,32,8,256]{3,2,1,0:T(8,128)} %bitcast_dynamic-update-slice_fusion.13, f32[16,256,256]{2,1,0:T(8,128)} %param.4), kind=kLoop, calls=%fused_computation.22 | loop fusion | flops 720896 | bytes 1572864
  61.3 1.7 bitcast_dynamic-update-slice_fusion.11
  63.0 0.8 bitcast_dynamic-update-slice_fusion.10
  63.8 0.8 bitcast_dynamic-update-slice_fusion.9
  64.5 0.8 bitcast_dynamic-update-slice_fusion.8
  65.3 0.7 bitcast_dynamic-update-slice_fusion.7
  66.1 0.8 bitcast_dynamic-update-slice_fusion.6
  66.8 0.7 bitcast_dynamic-update-slice_fusion.5
  67.6 0.8 bitcast_dynamic-update-slice_fusion.4
  68.4 0.8 bitcast_dynamic-update-slice_fusion.3
  69.1 0.8 bitcast_dynamic-update-slice_fusion.2
  69.9 1.7 bitcast_dynamic-update-slice_fusion.1
  71.6 1.8 %bitcast_dynamic-update-slice_fusion.refs_1_ = f32[16,32,8,256]{3,2,1,0:T(8,128)} fusion(f32[16,32,8,256]{3,2,1,0:T(8,128)} %bitcast_dynamic-update-slice_fusion.1, f32[16,256,256]{2,1,0:T(8,128)} %param.4, f32[1,256,256]{2,1,0:T(8,128)S(1)} %get-tuple-element.22), kind=kLoop, calls=%fused_computation.10 | loop fusion | flops 393216 | bytes 1048576 | tf_op jit(solution)/shard_map/stack | solution.py:210
  73.5 0.7 collective-permute-start.12
  74.2 2.4 %collective-permute-start.11 = (f32[16,32,256]{2,1,0:T(8,128)}, f32[16,32,256]{2,1,0:T(8,128)S(1)}, u32[]{:S(2)}, u32[]{:S(2)}) collective-permute-start(f32[16,32,256]{2,1,0:T(8,128)} %constant_dynamic-slice_fusion.18), channel_id=1, source_target_pairs={{0,6},{1,7},{2,4},{3,5},{4,2},{5,3},{6,0},{7,1},{8,14},{9,15},{10,... | collective-permute-start | bytes 1572872 | tf_op jit(solution)/shard_map/ppermute | solution.py:274
  76.6 1.0 broadcast_select_fusion
  78.3 1.3 collective-permute-start.3
  79.6 5.2 %collective-permute-start.2 = (f32[40,256]{1,0:T(8,128)}, f32[40,256]{1,0:T(8,128)}, u32[]{:S(2)}, u32[]{:S(2)}) collective-permute-start(f32[40,256]{1,0:T(8,128)} %select_maximum_fusion.13), channel_id=1, source_target_pairs={{0,8},{8,16},{16,24},{1,9},{9,17},{17,25},{2,10},{10,18},{18,26},{... | collective-permute-start | bytes 122888 | tf_op jit(solution)/shard_map/ppermute | solution.py:290
  84.7 1.0 add.440
  85.8 0.8 pad_maximum_fusion.3
  87.2 1.9 %pad_maximum_fusion = f32[568,256]{1,0:T(8,128)} fusion(f32[56,256]{1,0:T(8,128)S(1)} %get-tuple-element.64, f32[512,256]{1,0:T(8,128)} %bitcast.131), kind=kLoop, calls=%fused_computation.6 | loop fusion | flops 145408 | bytes 1163264 | tf_op jit(solution)/shard_map/concatenate | solution.py:328
  89.1 4.0 %collective-permute-start.7 = (f32[568,256]{1,0:T(8,128)}, f32[568,256]{1,0:T(8,128)}, u32[]{:S(2)}, u32[]{:S(2)}) collective-permute-start(f32[568,256]{1,0:T(8,128)} %pad_maximum_fusion), channel_id=1, source_target_pairs={{0,1},{1,0},{2,3},{3,2},{4,5},{5,4},{6,7},{7,6},{8,9},{9,8},{10,11... | collective-permute-start | bytes 1744904 | tf_op jit(solution)/shard_map/ppermute | solution.py:274
  93.2 1.9 %pad_maximum_fusion.2 = f32[568,256]{1,0:T(8,128)} fusion(f32[56,256]{1,0:T(8,128)S(1)} %get-tuple-element.62, f32[512,256]{1,0:T(8,128)} %bitcast.130), kind=kLoop, calls=%fused_computation.8 | loop fusion | flops 145408 | bytes 1163264 | tf_op jit(solution)/shard_map/concatenate | solution.py:328
  95.1 1.9 %pad_maximum_fusion.1 = f32[568,256]{1,0:T(8,128)} fusion(f32[56,256]{1,0:T(8,128)S(1)} %get-tuple-element.63, f32[512,256]{1,0:T(8,128)} %bitcast.129), kind=kLoop, calls=%fused_computation.7 | loop fusion | flops 145408 | bytes 1163264 | tf_op jit(solution)/shard_map/concatenate | solution.py:328
  97.2 1.0 collective-permute-start.8
  98.7 0.8 slice.418
  99.5 4.8 %fusion.refs_0_ = f32[16,34,8,256]{3,2,1,0:T(8,128)} fusion(f32[16,2,256]{2,1,0:T(2,128)S(1)} %reshape.133, f32[16,2,256]{2,1,0:T(2,128)S(1)} %reshape.131, f32[16,256,256]{2,1,0:T(8,128)} %add_divide_fusion.cells), kind=kLoop, calls=%fused_computation.1 | loop fusion | flops 6684672 | bytes 8716288 | tf_op jit(solution)/shard_map/reshape | solution.py:294
  105.0 2.4 %collective-permute-start.10 = (f32[16,32,256]{2,1,0:T(8,128)}, f32[16,32,256]{2,1,0:T(8,128)}, u32[]{:S(2)}, u32[]{:S(2)}) collective-permute-start(f32[16,32,256]{2,1,0:T(8,128)} %constant_dynamic-slice_fusion.19), channel_id=1, source_target_pairs={{0,7},{1,6},{2,5},{3,4},{4,3},{5,2},{6,1},{7,0},{8,15},{9,14},{10,... | collective-permute-start | bytes 1572872 | tf_op jit(solution)/shard_map/ppermute | solution.py:274
  107.4 0.8 slice_bitcast_fusion.2
  108.2 15.7 %collective-permute-done.8 = f32[568,256]{1,0:T(8,128)} collective-permute-done((f32[568,256]{1,0:T(8,128)}, f32[568,256]{1,0:T(8,128)}, u32[]{:S(2)}, u32[]{:S(2)}) %collective-permute-start.8) | collective-permute-done | bytes 581664 | tf_op jit(solution)/shard_map/ppermute | solution.py:274
  123.9 0.8 slice_bitcast_fusion.1
  124.7 22.7 %collective-permute-done.9 = f32[568,256]{1,0:T(8,128)} collective-permute-done((f32[568,256]{1,0:T(8,128)}, f32[568,256]{1,0:T(8,128)}, u32[]{:S(2)}, u32[]{:S(2)}) %collective-permute-start.9) | collective-permute-done | bytes 581664 | tf_op jit(solution)/shard_map/ppermute | solution.py:274
  147.4 0.8 slice_bitcast_fusion
  148.9 0.7 fusion.51
  150.9 0.7 fusion.49
  151.8 1.1 slice.468
  153.0 1.4 reshape.151
  154.4 1.4 reshape.152
  155.7 1.2 slice.469
  157.0 1.3 slice.470
  158.4 0.8 fusion.3
  159.3 2.2 %copy-done.1 = f32[16,32,8,256]{3,2,1,0:T(8,128)S(1)} copy-done((f32[16,32,8,256]{3,2,1,0:T(8,128)S(1)}, f32[16,32,8,256]{3,2,1,0:T(8,128)}, u32[]{:S(2)}) %copy-start.1) | copy-done | bytes 4194328
  161.4 9.6 %shard_map.39.refs_10_ = f32[16,32,8,256]{3,2,1,0:T(8,128)} custom-call(f32[16,34,8,256]{3,2,1,0:T(8,128)S(1)} %copy-done, f32[16,32,8,256]{3,2,1,0:T(8,128)S(1)} %copy-done.1, f32[34,8,128]{2,1,0:T(8,128)S(1)} %bitcast.122, f32[34,8,128]{2,1,0:T(8,128)S(1)} %fusion.1.refs_3_, f32[16,17,8,256]{3,2,1,0:T(8,128)S(1)} %bitcast.120), custom_call_target="tpu_custom_call" | custom-call | flops 9830400 | bytes 7864320 | tf_op jit(solution)/shard_map/pallas_call | solution.py:177
  171.1 10.9 %shard_map.40 = f32[16,32,8,256]{3,2,1,0:T(8,128)} custom-call(f32[16,34,8,256]{3,2,1,0:T(8,128)S(1)} %copy-done, f32[16,32,8,256]{3,2,1,0:T(8,128)S(1)} %copy-done.1, f32[34,8,128]{2,1,0:T(8,128)S(1)} %bitcast.123, f32[34,8,128]{2,1,0:T(8,128)S(1)} %fusion.1.refs_3_, ...), custom_call_target="tpu_custom_call", output_to_operand_aliasing={{}: (10, {})} | custom-call | flops 11141120 | bytes 8912896 | tf_op jit(solution)/shard_map/pallas_call | solution.py:177
  (94 shorter events, 6.5 us)
Async XLA Ops:
  16.8 56.7 %collective-permute-start.1 = (f32[256,128]{1,0:T(8,128)}, f32[256,128]{1,0:T(8,128)}, u32[]{:S(2)}, u32[]{:S(2)}) collective-permute-start(f32[256,128]{1,0:T(8,128)} %bitcast.132), channel_id=1, source_target_pairs={{1,0},{2,1},{3,2},{4,3},{5,4},{6,5},{7,6},{9,8},{10,9},{11,10},{12... | collective-permute-start | bytes 393224 | tf_op jit(solution)/shard_map/ppermute | solution.py:286
  18.1 56.1 %collective-permute-start = (f32[256,128]{1,0:T(8,128)}, f32[256,128]{1,0:T(8,128)}, u32[]{:S(2)}, u32[]{:S(2)}) collective-permute-start(f32[256,128]{1,0:T(8,128)} %bitcast.133), channel_id=1, source_target_pairs={{0,1},{1,2},{2,3},{3,4},{4,5},{5,6},{6,7},{8,9},{9,10},{10,11},{11... | collective-permute-start | bytes 393224 | tf_op jit(solution)/shard_map/ppermute | solution.py:285
  34.7 51.1 %collective-permute-start.4 = (f32[4,8,256]{2,1,0:T(8,128)}, f32[4,8,256]{2,1,0:T(8,128)}, u32[]{:S(2)}, u32[]{:S(2)}) collective-permute-start(f32[4,8,256]{2,1,0:T(8,128)} %get-tuple-element.86), channel_id=1, source_target_pairs={{0,4},{1,5},{2,6},{3,7},{4,0},{5,1},{6,2},{7,3},{8,12},{9,13},{10,... | collective-permute-start | bytes 98312 | tf_op jit(solution)/shard_map/ppermute | solution.py:274
  40.8 37.4 %collective-permute-start.6 = (f32[4,40,256]{2,1,0:T(8,128)}, f32[4,40,256]{2,1,0:T(8,128)}, u32[]{:S(2)}, u32[]{:S(2)}) collective-permute-start(f32[4,40,256]{2,1,0:T(8,128)} %get-tuple-element.60), channel_id=1, source_target_pairs={{7,11},{8,4},{15,19},{16,12},{23,27},{24,20}} | collective-permute-start | bytes 491528 | tf_op jit(solution)/shard_map/ppermute | solution.py:313
  42.1 37.4 %collective-permute-start.5 = (f32[4,40,256]{2,1,0:T(8,128)S(1)}, f32[4,40,256]{2,1,0:T(8,128)}, u32[]{:S(2)}, u32[]{:S(2)}) collective-permute-start(f32[4,40,256]{2,1,0:T(8,128)S(1)} %get-tuple-element.61), channel_id=1, source_target_pairs={{7,15},{8,0},{15,23},{16,8},{23,31},{24,16}} | collective-permute-start | bytes 491528 | tf_op jit(solution)/shard_map/ppermute | solution.py:313
  55.4 7.7 %copy-start.2 = (f32[16,256,256]{2,1,0:T(8,128)S(1)}, f32[16,256,256]{2,1,0:T(8,128)}, u32[]{:S(2)}) copy-start(f32[16,256,256]{2,1,0:T(8,128)} %param.4) | copy-start | bytes 12582916
  73.5 97.6 %collective-permute-start.12 = (f32[16,32,256]{2,1,0:T(8,128)}, f32[16,32,256]{2,1,0:T(8,128)S(1)}, u32[]{:S(2)}, u32[]{:S(2)}) collective-permute-start(f32[16,32,256]{2,1,0:T(8,128)} %constant_dynamic-slice_fusion.17), channel_id=1, source_target_pairs={{0,5},{1,4},{2,7},{3,6},{4,1},{5,0},{6,3},{7,2},{8,13},{9,12},{10,... | collective-permute-start | bytes 1572872 | tf_op jit(solution)/shard_map/ppermute | solution.py:274
  74.2 96.9 %collective-permute-start.11 = (f32[16,32,256]{2,1,0:T(8,128)}, f32[16,32,256]{2,1,0:T(8,128)S(1)}, u32[]{:S(2)}, u32[]{:S(2)}) collective-permute-start(f32[16,32,256]{2,1,0:T(8,128)} %constant_dynamic-slice_fusion.18), channel_id=1, source_target_pairs={{0,6},{1,7},{2,4},{3,5},{4,2},{5,3},{6,0},{7,1},{8,14},{9,15},{10,... | collective-permute-start | bytes 1572872 | tf_op jit(solution)/shard_map/ppermute | solution.py:274
  77.6 8.2 %copy-start.3 = (f32[256,128]{1,0:T(8,128)}, f32[256,128]{1,0:T(8,128)S(1)}, u32[]{:S(2)}) copy-start(f32[256,128]{1,0:T(8,128)S(1)} %broadcast_select_fusion) | copy-start | bytes 393220
  78.3 18.9 %collective-permute-start.3 = (f32[40,256]{1,0:T(8,128)S(1)}, f32[40,256]{1,0:T(8,128)S(1)}, u32[]{:S(2)}, u32[]{:S(2)}) collective-permute-start(f32[40,256]{1,0:T(8,128)S(1)} %select_maximum_fusion.12), channel_id=1, source_target_pairs={{8,0},{16,8},{24,16},{9,1},{17,9},{25,17},{10,2},{18,10},{26,18},{... | collective-permute-start | bytes 122888 | tf_op jit(solution)/shard_map/ppermute | solution.py:291
  79.6 18.6 %collective-permute-start.2 = (f32[40,256]{1,0:T(8,128)}, f32[40,256]{1,0:T(8,128)}, u32[]{:S(2)}, u32[]{:S(2)}) collective-permute-start(f32[40,256]{1,0:T(8,128)} %select_maximum_fusion.13), channel_id=1, source_target_pairs={{0,8},{8,16},{16,24},{1,9},{9,17},{17,25},{2,10},{10,18},{18,26},{... | collective-permute-start | bytes 122888 | tf_op jit(solution)/shard_map/ppermute | solution.py:290
  89.1 15.9 %collective-permute-start.7 = (f32[568,256]{1,0:T(8,128)}, f32[568,256]{1,0:T(8,128)}, u32[]{:S(2)}, u32[]{:S(2)}) collective-permute-start(f32[568,256]{1,0:T(8,128)} %pad_maximum_fusion), channel_id=1, source_target_pairs={{0,1},{1,0},{2,3},{3,2},{4,5},{5,4},{6,7},{7,6},{8,9},{9,8},{10,11... | collective-permute-start | bytes 1744904 | tf_op jit(solution)/shard_map/ppermute | solution.py:274
  97.2 26.7 %collective-permute-start.8 = (f32[568,256]{1,0:T(8,128)}, f32[568,256]{1,0:T(8,128)}, u32[]{:S(2)}, u32[]{:S(2)}) collective-permute-start(f32[568,256]{1,0:T(8,128)} %pad_maximum_fusion.1), channel_id=1, source_target_pairs={{0,2},{1,3},{2,0},{3,1},{4,6},{5,7},{6,4},{7,5},{8,10},{9,11},{10,... | collective-permute-start | bytes 1744904 | tf_op jit(solution)/shard_map/ppermute | solution.py:274
  98.2 49.2 %collective-permute-start.9 = (f32[568,256]{1,0:T(8,128)}, f32[568,256]{1,0:T(8,128)}, u32[]{:S(2)}, u32[]{:S(2)}) collective-permute-start(f32[568,256]{1,0:T(8,128)} %pad_maximum_fusion.2), channel_id=1, source_target_pairs={{0,3},{1,2},{2,1},{3,0},{4,7},{5,6},{6,5},{7,4},{8,11},{9,10},{10,... | collective-permute-start | bytes 1744904 | tf_op jit(solution)/shard_map/ppermute | solution.py:274
  99.5 5.5 %copy-start.4 = (f32[256,128]{1,0:T(8,128)S(1)}, f32[256,128]{1,0:T(8,128)}, u32[]{:S(2)}) copy-start(f32[256,128]{1,0:T(8,128)} %copy-done.3) | copy-start | bytes 393220
  99.5 48.7 %copy-start.5 = (f32[1,40,256]{2,1,0:T(8,128)S(1)}, f32[1,40,256]{2,1,0:T(8,128)}, u32[]{:S(2)}) copy-start(f32[1,40,256]{2,1,0:T(8,128)} %constant_dynamic-slice_fusion.25) | copy-start | bytes 122884
  105.0 66.1 %collective-permute-start.10 = (f32[16,32,256]{2,1,0:T(8,128)}, f32[16,32,256]{2,1,0:T(8,128)}, u32[]{:S(2)}, u32[]{:S(2)}) collective-permute-start(f32[16,32,256]{2,1,0:T(8,128)} %constant_dynamic-slice_fusion.19), channel_id=1, source_target_pairs={{0,7},{1,6},{2,5},{3,4},{4,3},{5,2},{6,1},{7,0},{8,15},{9,14},{10,... | collective-permute-start | bytes 1572872 | tf_op jit(solution)/shard_map/ppermute | solution.py:274
  123.9 47.2 %collective-permute-start.13 = (f32[16,32,256]{2,1,0:T(8,128)}, f32[16,32,256]{2,1,0:T(8,128)}, u32[]{:S(2)}, u32[]{:S(2)}) collective-permute-start(f32[16,32,256]{2,1,0:T(8,128)} %get-tuple-element.18), channel_id=1, source_target_pairs={{0,4},{1,5},{2,6},{3,7},{4,0},{5,1},{6,2},{7,3},{8,12},{9,13},{10,... | collective-permute-start | bytes 1572872 | tf_op jit(solution)/shard_map/ppermute | solution.py:274
  155.7 3.5 %copy-start = (f32[16,34,8,256]{3,2,1,0:T(8,128)S(1)}, f32[16,34,8,256]{3,2,1,0:T(8,128)}, u32[]{:S(2)}) copy-start(f32[16,34,8,256]{3,2,1,0:T(8,128)} %fusion.refs_0_) | copy-start | bytes 13369348
  159.2 2.2 %copy-start.1 = (f32[16,32,8,256]{3,2,1,0:T(8,128)S(1)}, f32[16,32,8,256]{3,2,1,0:T(8,128)}, u32[]{:S(2)}) copy-start(f32[16,32,8,256]{3,2,1,0:T(8,128)} %bitcast_dynamic-update-slice_fusion.refs_1_) | copy-start | bytes 12582916

commit v2 on v0

v2 whole, which is shorter than its diff:
```python
import functools

import jax
import jax.numpy as jnp
from jax import lax
from jax.experimental import pallas as pl
from jax.experimental.pallas import tpu as pltpu
from jax.sharding import PartitionSpec as P

LANES = 128
SLOT = 8
GROUP = 8
MIB = 1024 * 1024

ANYWHERE = pl.BlockSpec(memory_space=pl.ANY)
WHOLE = pl.BlockSpec(memory_space=pltpu.VMEM)


def f32(*shape):
    return jax.ShapeDtypeStruct(shape, jnp.float32)


def lanes_of(rows):
    return lax.broadcasted_iota(jnp.int32, (rows, LANES), 1)


def packed_layer(first, last, layer):
    both = jnp.where(lanes_of(first.shape[0]) < LANES // 2, first, last)
    return pltpu.roll(both, (layer * SLOT + 4) % LANES, 1)


def sides_of(first, last, target, count):
    layers, depth, _, _ = first.shape
    rows = depth * GROUP
    lane = lanes_of(rows)
    place = lane % SLOT
    kept = ((place == 2) | (place == 3)) & (target > 0) | ((place == 4) | (place == 5)) & (target < count - 1)
    total = jnp.zeros((rows, LANES), jnp.float32)
    for layer in range(layers):
        turned = packed_layer(first[layer].reshape(rows, LANES), last[layer].reshape(rows, LANES), layer)
        total = jnp.where((lane // SLOT == layer) & kept, turned, total)
    return total


def fold_into(thin, packed):
    rows = packed.shape[0]
    wide = thin.shape[2] // LANES
    both = packed[: rows // 2] + pltpu.roll(packed[rows // 2 :], 4, 1)
    thin[...] = jnp.zeros(thin.shape, jnp.float32)
    for i in range(rows // 2 // GROUP):
        thin[i // wide, :, i % wide * LANES : (i % wide + 1) * LANES] = both[i * GROUP : (i + 1) * GROUP]


def unfold_into(packed, first, thin, rows):
    wide = thin.shape[2] // LANES
    for i in range(rows // 2 // GROUP):
        both = thin[i // wide, :, i % wide * LANES : (i % wide + 1) * LANES]
        packed[pl.ds(pl.multiple_of(first + i * GROUP, GROUP), GROUP), :] = both
        packed[pl.ds(pl.multiple_of(first + rows // 2 + i * GROUP, GROUP), GROUP), :] = pltpu.roll(both, LANES - 4, 1)


def strip_of(message, layers, depth):
    return message.at[pl.ds(0, layers * depth)].reshape(layers, depth, GROUP, message.shape[2])


def message_kernel(parts, tips, count, noise, *refs):
    outs = refs[: len(parts)]
    left, right, thin, rows_of, sems = refs[-5:]
    layers, depth, _, width = noise.shape
    columns = width // count
    me = lax.axis_index("ay")
    sided = [(s, part[0]) for s, part in enumerate(parts) if part[3]]
    copies = []
    for i, (s, step) in enumerate(sided):
        target = me ^ step
        at_left = pl.multiple_of(jnp.maximum(target, 1) * columns - LANES, LANES)
        at_right = pl.multiple_of(jnp.minimum(target + 1, count - 1) * columns, LANES)
        copies.append(
            [
                pltpu.make_async_copy(noise.at[:, :, :, pl.ds(at_left, LANES)], left.at[i], sems.at[0, s]),
                pltpu.make_async_copy(noise.at[:, :, :, pl.ds(at_right, LANES)], right.at[i], sems.at[1, s]),
            ]
        )
    for pair in copies:
        for copy in pair:
            copy.start()
    ends = []
    is_first = me == 0
    for i, step in enumerate(tips):
        at = pl.multiple_of((me ^ step) * columns, LANES)
        group = noise.at[:, jnp.where(is_first, 0, depth - 1), :, pl.ds(at, columns)]
        ends.append(pltpu.make_async_copy(group, rows_of.at[i], sems.at[4, i]))
        ends[-1].start()
    tip_copies = ends[:]
    ends = []
    for s, (step, lower, size, _) in enumerate(parts):
        at = pl.multiple_of((me ^ step) * columns, LANES)
        if size:
            piece = noise.at[pl.ds(lower, size), :, :, pl.ds(at, columns)]
            ends.append(pltpu.make_async_copy(piece, strip_of(outs[s], size, depth), sems.at[2, s]))
            ends[-1].start()
    for i, (s, step) in enumerate(sided):
        for copy in copies[i]:
            copy.wait()
        sides = sides_of(right.at[i], left.at[i], me ^ step, count)
        fold_into(thin.at[i], sides)
        if step in tips:
            at = tips.index(step)
            tip_copies[at].wait()
            tip = refs[len(parts)]
            base = at * (2 * layers + GROUP)
            for layer in range(layers):
                group = rows_of[at, layer]
                tip[base + 2 * layer : base + 2 * layer + 2, :] = jnp.where(is_first, group[:2], group[GROUP - 2 :])
            end = base + 2 * layers
            tip[end : end + GROUP, :] = jnp.zeros((GROUP, columns), jnp.float32)
            tip[end : end + 1, :LANES] = jnp.where(is_first, sides[:1], sides[-1:])
        to = outs[s].at[pl.ds(parts[s][2] * depth, thin.shape[1])]
        ends.append(pltpu.make_async_copy(thin.at[i], to, sems.at[3, s]))
        ends[-1].start()
    for end in ends:
        end.wait()


def messages(noise, parts, count, tips=()):
    layers, depth, _, width = noise.shape
    columns = width // count
    lines = -(-depth // 2 // (columns // LANES))
    shapes = [f32(part[2] * depth + (lines if part[3] else 0), GROUP, columns) for part in parts]
    block = functools.partial(pltpu.VMEM, dtype=jnp.float32)
    sided = sum(part[3] for part in parts)
    shapes += [f32(len(tips) * (2 * layers + GROUP), columns)] if tips else []
    tile = (sided, layers, depth, GROUP, LANES)
    return pl.pallas_call(
        functools.partial(message_kernel, parts, tips, count),
        in_specs=[ANYWHERE],
        out_specs=[ANYWHERE] * len(parts) + [WHOLE] * (len(shapes) - len(parts)),
        out_shape=shapes,
        scratch_shapes=[
            block(tile),
            block(tile),
            block((sided, lines, GROUP, columns)),
            block((max(1, len(tips)), layers, GROUP, columns)),
            pltpu.SemaphoreType.DMA((5, max(len(parts), len(tips)))),
        ],
        compiler_params=pltpu.CompilerParams(vmem_limit_bytes=16 * MIB),
    )(noise)


def factor_kernel(kappa, mask, inverse, pivots, packed):
    layers, rows, columns = kappa.shape
    lane = lanes_of(rows)
    active = mask[...].astype(jnp.float32)
    total = jnp.zeros((rows, LANES), jnp.float32)
    pivot = jnp.zeros((rows, columns), jnp.float32)
    for layer in range(layers):
        value = kappa[layer]
        scale = active / (6.0 + value)
        inverse[layer] = scale
        pivot = 1.0 / (2.5 + value - pivot)
        pivots[layer] = pivot
        turned = packed_layer(scale[:, :LANES], scale[:, columns - LANES :], layer)
        total = jnp.where(lane // SLOT == layer, turned, total)
    packed[...] = total


def coefficients(kappa, mask, rows=32):
    layers, height, columns = kappa.shape
    block = pl.BlockSpec((layers, rows, columns), lambda r: (0, r, 0))
    return pl.pallas_call(
        factor_kernel,
        grid=(height // rows,),
        in_specs=[block, pl.BlockSpec((rows, columns), lambda r: (r, 0))],
        out_specs=[block, block, pl.BlockSpec((rows, LANES), lambda r: (r, 0))],
        out_shape=[f32(*kappa.shape), f32(*kappa.shape), f32(height, LANES)],
        compiler_params=pltpu.CompilerParams(vmem_limit_bytes=16 * MIB),
    )(kappa, mask)


def chunks(groups, size=4):
    return [(first, min(size, groups - first)) for first in range(0, groups, size)]


def around(cells, sides, layer, first, rows):
    tiles = cells.shape[1]
    lane = lanes_of(rows)
    side = pltpu.roll(sides[pl.ds(first - GROUP, rows), :], LANES - 3 - layer * SLOT, 1)
    centre = [cells[layer + 1, t, pl.ds(first, rows), :] for t in range(tiles)]
    left = [pltpu.roll(x, 1, 1) for x in centre]
    right = [pltpu.roll(x, LANES - 1, 1) for x in centre]
    totals = []
    for t in range(tiles):
        total = cells[layer + 1, t, pl.ds(first + 1, rows), :] + cells[layer + 1, t, pl.ds(first - 1, rows), :]
        total = total + jnp.where(lane == 0, side if t == 0 else left[t - 1], left[t])
        total = total + jnp.where(lane == LANES - 1, side if t == tiles - 1 else right[t + 1], right[t])
        totals.append(total + cells[layer, t, pl.ds(first, rows), :] + cells[layer + 2, t, pl.ds(first, rows), :])
    return totals


def solve(noise, inverse, pivots, base, packed_noise, packed_inverse, initial, middle, forward, packed, wait_pivots, finished, unroll=1):
    layers, columns = noise.shape[0], noise.shape[3]
    groups = forward.shape[1]
    span = groups + 2
    rows = span * GROUP
    tiles = columns // LANES
    own, sides, sides_middle = packed
    for cells in (initial, middle):
        cells[0] = jnp.zeros(cells.shape[1:], jnp.float32)
        cells[layers + 1] = jnp.zeros(cells.shape[1:], jnp.float32)
    forward[0] = jnp.zeros(forward.shape[1:], jnp.float32)
    forward[layers + 1] = jnp.zeros(forward.shape[1:], jnp.float32)
    own[...] = jnp.zeros(own.shape, jnp.float32)

    def first_step(layer, carry):
        for first, size in chunks(span):
            height = size * GROUP
            lane = lanes_of(height)
            at = pl.ds(base + first, size)
            field = (inverse[layer, at] * noise[layer, at]).reshape(height, columns)
            for t in range(tiles):
                initial[layer + 1, t, pl.ds((first + 1) * GROUP, height), :] = field[:, t * LANES : (t + 1) * LANES]
            both = jnp.where(lane == LANES - 1, field[:, columns - LANES :], field[:, :LANES])
            turned = pltpu.roll(both, layer * SLOT + 1, 1)
            here = pl.ds(first * GROUP, height)
            own[here, :] = jnp.where(lane // SLOT == layer, turned, own[here, :])
        return carry

    lax.fori_loop(0, layers, first_step, 0, unroll=unroll)

    lane = lanes_of(rows)
    place = lane % SLOT
    side = jnp.where(place < 2, own[...], packed_inverse * packed_noise)
    total = jnp.where(lane >= SLOT, pltpu.roll(side, SLOT, 1), 0.0)
    total = total + jnp.where(lane < LANES - SLOT, pltpu.roll(side, LANES - SLOT, 1), 0.0)
    total = total + pltpu.roll(side, 1, 0) + pltpu.roll(side, rows - 1, 0)
    total = total + jnp.where(
        place == 3,
        pltpu.roll(side, 1, 1) + pltpu.roll(side, 2, 1),
        pltpu.roll(side, LANES - 1, 1) + pltpu.roll(side, 4, 1),
    )
    side_middle = packed_inverse * (packed_noise + total)
    sides[...] = jnp.where(place == 2, pltpu.roll(side, LANES - 2, 1), side)
    sides_middle[...] = jnp.where(place == 2, pltpu.roll(side_middle, LANES - 2, 1), side_middle)

    def second_step(layer, carry):
        for first, size in chunks(span):
            height = size * GROUP
            at = pl.ds(base + first, size)
            totals = around(initial, sides, layer, (first + 1) * GROUP, height)
            for t in range(tiles):
                part = pl.ds(t * LANES, LANES)
                field = inverse[layer, at, :, part] * (noise[layer, at, :, part] + totals[t].reshape(size, GROUP, LANES))
                middle[layer + 1, t, pl.ds((first + 1) * GROUP, height), :] = field.reshape(height, LANES)
        return carry

    lax.fori_loop(0, layers, second_step, 0, unroll=unroll)
    wait_pivots()

    def third_step(layer, carry):
        for first, size in chunks(groups):
            height = size * GROUP
            at = pl.ds(base + 1 + first, size)
            here = pl.ds(first, size)
            totals = around(middle, sides_middle, layer, (first + 2) * GROUP, height)
            for t in range(tiles):
                part = pl.ds(t * LANES, LANES)
                field = inverse[layer, at, :, part] * (noise[layer, at, :, part] + totals[t].reshape(size, GROUP, LANES))
                pivot = pivots[layer, pl.ds(base + first, size), :, part]
                forward[layer + 1, here, :, part] = (field + forward[layer, here, :, part]) * pivot
        return carry

    lax.fori_loop(0, layers, third_step, 0, unroll=unroll)

    def last_step(step, carry):
        layer = layers - 1 - step
        for first, size in chunks(groups):
            here = pl.ds(first, size)
            pivot = pivots[layer, pl.ds(base + first, size)]
            forward[layer + 1, here] = forward[layer + 1, here] + pivot * forward[layer + 2, here]
        finished(layer)
        return carry

    lax.fori_loop(0, layers, last_step, 0, unroll=unroll)


def solve_scratch(layers, groups, columns):
    block = functools.partial(pltpu.VMEM, dtype=jnp.float32)
    padded = (layers + 2, columns // LANES, (groups + 4) * GROUP, LANES)
    rows = (groups + 2) * GROUP
    return [
        block(padded),
        block(padded),
        block((layers + 2, groups, GROUP, columns)),
        block((rows, LANES)),
        block((rows, LANES)),
        block((rows, LANES)),
    ]


def merged_sides(paired, other):
    odd = lax.axis_index("ay") % 2
    is_left = (lanes_of(paired.shape[0]) % SLOT < 4).astype(jnp.int32)
    return jnp.where(is_left == odd, paired, other)


def last_two(half):
    me = lax.axis_index("ay")
    one, other = me ^ half, me ^ (half + 1)
    return jnp.minimum(one, other), one, other


def block_kernel(half, depth, *refs):
    known = 2 * half - 3
    inverse_in, pivots_in, own_piece, own_sides = refs[:4]
    pieces = refs[4 : 4 + known]
    paired, other, above, below = refs[4 + known : 8 + known]
    out, noise_out, inverse_out, pivots_out, packed_noise, packed_inverse = refs[8 + known : 14 + known]
    noise, inverse, pivots, thin, *scratch, sems, out_sems = refs[14 + known :]
    initial, middle, forward, own, sides, sides_middle = scratch
    layers, groups, _, columns = pivots_in.shape
    rows, height, lines = depth * GROUP, groups * GROUP, thin.shape[1]
    me = lax.axis_index("ay")
    last = last_two(half)[0] * depth
    steps = [0] + [step for step in range(2 * half - 1, 0, -1) if step not in (half, half + 1)]

    inverse_copy = pltpu.make_async_copy(inverse_in, inverse.at[:, pl.ds(2, groups)], sems.at[0])
    pivot_copy = pltpu.make_async_copy(pivots_in, pivots.at[:, pl.ds(1, groups)], sems.at[1])
    waits, thin_copies = [inverse_copy], []
    inverse_copy.start()
    for index, step in enumerate(steps):
        target = noise.at[:, pl.ds(2 + (me ^ step) * depth, depth)]
        if step:
            message = pieces[index - 1]
            piece = strip_of(message, layers, depth)
            side = message.at[pl.ds(layers * depth, lines)]
        else:
            piece = own_piece.at[:, :, :, pl.ds(pl.multiple_of(me * columns, LANES), columns)]
            side = own_sides
        waits.append(pltpu.make_async_copy(piece, target, sems.at[2 + index]))
        waits[-1].start()
        thin_copies.append(pltpu.make_async_copy(side, thin.at[index], sems.at[2 + len(steps) + index]))
        thin_copies[-1].start()
    pivot_copy.start()

    nothing = jnp.zeros((layers, GROUP, columns), jnp.float32)
    for ref in (noise, inverse):
        for group in (0, 1, groups + 2, groups + 3):
            ref[:, group] = nothing
    pivots[:, 0] = nothing
    pivots[:, groups + 1] = nothing
    packed_noise[...] = jnp.zeros(packed_noise.shape, jnp.float32)
    packed_inverse[...] = jnp.zeros(packed_inverse.shape, jnp.float32)
    packed_inverse[2 * GROUP : 2 * GROUP + height] = merged_sides(paired[...], other[...])
    end = 4 * layers
    for message, group, place, row in ((above, 1, GROUP - 2, 2 * GROUP - 1), (below, groups + 2, 0, 2 * GROUP + height)):
        for layer in range(layers):
            noise[layer, group, place : place + 2, :] = message[2 * layer : 2 * layer + 2, :]
            inverse[layer, group, place : place + 2, :] = message[2 * (layers + layer) : 2 * (layers + layer) + 2, :]
        packed_noise[row : row + 1] = message[end : end + 1, :LANES]
        packed_inverse[row : row + 1] = message[end : end + 1, LANES : 2 * LANES]
    for index, step in enumerate(steps):
        thin_copies[index].wait()
        unfold_into(packed_noise, 2 * GROUP + (me ^ step) * rows, thin.at[index], rows)
    for copy in waits:
        copy.wait()
    windows = [
        pltpu.make_async_copy(noise.at[:, pl.ds(last, 2)], noise_out.at[:, pl.ds(0, 2)], sems.at[0]),
        pltpu.make_async_copy(noise.at[:, pl.ds(last + 2 * depth + 2, 2)], noise_out.at[:, pl.ds(2, 2)], sems.at[2]),
        pltpu.make_async_copy(inverse.at[:, pl.ds(last, 2 * depth + 4)], inverse_out, sems.at[3]),
    ]
    for copy in windows:
        copy.start()
    pivot_window = pltpu.make_async_copy(pivots.at[:, pl.ds(last, 2 * depth + 2)], pivots_out, sems.at[6])

    def wait_pivots():
        pivot_copy.wait()
        pivot_window.start()

    def place_out(layer):
        return pltpu.make_async_copy(forward.at[layer + 1], out.at[layer], out_sems.at[layer])

    inner = pl.ds(GROUP, height + 2 * GROUP)
    solve(
        noise, inverse, pivots, 1, packed_noise[inner, :], packed_inverse[inner, :],
        initial, middle, forward, (own, sides, sides_middle), wait_pivots, lambda layer: place_out(layer).start(),
    )
    for layer in range(layers):
        place_out(layer).wait()
    for copy in windows:
        copy.wait()
    pivot_window.wait()


def solve_block(inverse, pivots, own_piece, own_sides, pieces, paired, other, above, below, half, depth):
    layers, groups, _, columns = pivots.shape
    block = functools.partial(pltpu.VMEM, dtype=jnp.float32)
    packed = f32((groups + 4) * GROUP, LANES)
    return pl.pallas_call(
        functools.partial(block_kernel, half, depth),
        in_specs=[ANYWHERE] * (4 + len(pieces)) + [WHOLE] * 4,
        out_specs=[ANYWHERE] * 4 + [WHOLE] * 2,
        out_shape=[
            f32(layers, groups, GROUP, columns),
            f32(layers, 4, GROUP, columns),
            f32(layers, 2 * depth + 4, GROUP, columns),
            f32(layers, 2 * depth + 2, GROUP, columns),
            packed,
            packed,
        ],
        scratch_shapes=[
            block((layers, groups + 4, GROUP, columns)),
            block((layers, groups + 4, GROUP, columns)),
            block((layers, groups + 2, GROUP, columns)),
            block((len(pieces) + 1, *own_sides.shape)),
            *solve_scratch(layers, groups, columns),
            pltpu.SemaphoreType.DMA((2 * len(pieces) + 7,)),
            pltpu.SemaphoreType.DMA((layers,)),
        ],
        compiler_params=pltpu.CompilerParams(vmem_limit_bytes=40 * MIB),
    )(inverse, pivots, own_piece, own_sides, *pieces, paired, other, above, below)


def edge_kernel(steps, count, own_piece, own_sides, inverse, paired, other, *refs):
    pieces, tips = refs[: len(steps) - 1], refs[len(steps) - 1 : len(steps) + 1]
    up, down, ends, thin, outer, sems = refs[len(steps) + 1 :]
    layers, columns = ends.shape[1], ends.shape[3]
    depth, lines = own_piece.shape[1], thin.shape[1]
    height = paired.shape[0]
    half = count // 2
    wide = columns // LANES
    me = lax.axis_index("ay")
    copies = [
        pltpu.make_async_copy(inverse.at[:, 0], outer.at[0], sems.at[0]),
        pltpu.make_async_copy(inverse.at[:, inverse.shape[1] - 1], outer.at[1], sems.at[1]),
    ]
    for copy in copies:
        copy.start()

    def fetch(step, piece, side):
        if step:
            rows, sides = strip_of(piece, layers, depth), piece.at[pl.ds(layers * depth, lines)]
        else:
            rows, sides = own_piece.at[:, :, :, pl.ds(pl.multiple_of(me * columns, LANES), columns)], own_sides
        pltpu.make_async_copy(rows.at[:, side * (depth - 1)], ends.at[side], sems.at[2 + side]).start()
        pltpu.make_async_copy(sides, thin.at[side], sems.at[4 + side]).start()

    for step, piece in zip(steps, (None, *pieces)):
        for side in range(2):
            pl.when((me ^ step) == side * (count - 1))(functools.partial(fetch, step, piece, side))
    for copy in copies:
        copy.wait()
    for side, (out, place, row) in enumerate(((up, 0, 0), (down, GROUP - 2, height - 1))):
        target = side * (count - 1)
        late = ((me ^ half) == target) | ((me ^ (half + 1)) == target)

        def wait(side):
            pltpu.make_async_copy(ends.at[side], ends.at[side], sems.at[2 + side]).wait()
            pltpu.make_async_copy(thin.at[side], thin.at[side], sems.at[4 + side]).wait()

        pl.when(jnp.logical_not(late))(functools.partial(wait, side))
        tip = jnp.where((me ^ half) == target, tips[0][: 2 * layers + GROUP], tips[1][...])
        for layer in range(layers):
            out[2 * layer : 2 * layer + 2, :] = jnp.where(
                late, tip[2 * layer : 2 * layer + 2, :], ends[side, layer, place : place + 2, :]
            )
            out[2 * (layers + layer) : 2 * (layers + layer) + 2, :] = outer[side, layer, place : place + 2, :]
        if side:
            i = depth // 2 - 1
            both = thin[side, i // wide, :, i % wide * LANES : (i % wide + 1) * LANES]
            corner = pltpu.roll(both, LANES - 4, 1)[GROUP - 1 :]
        else:
            corner = thin[side, 0, 0:1, :LANES]
        end = 4 * layers
        out[end : end + GROUP, :] = jnp.zeros((GROUP, columns), jnp.float32)
        out[end : end + 1, :LANES] = jnp.where(late, tip[2 * layers : 2 * layers + 1, :LANES], corner)
        out[end : end + 1, LANES : 2 * LANES] = merged_sides(paired[row : row + 1, :], other[row : row + 1, :])


def edges(own_piece, own_sides, inverse, paired, other, steps, pieces, tips, count):
    layers, _, _, columns = inverse.shape
    outer = f32(4 * layers + GROUP, columns)
    block = functools.partial(pltpu.VMEM, dtype=jnp.float32)
    return pl.pallas_call(
        functools.partial(edge_kernel, steps, count),
        in_specs=[ANYWHERE] * 3 + [WHOLE] * 2 + [ANYWHERE] * len(pieces) + [WHOLE] * 2,
        out_specs=[WHOLE] * 2,
        out_shape=[outer, outer],
        scratch_shapes=[
            block((2, layers, GROUP, columns)),
            block((2, *own_sides.shape)),
            block((2, layers, GROUP, columns)),
            pltpu.SemaphoreType.DMA((6,)),
        ],
        compiler_params=pltpu.CompilerParams(vmem_limit_bytes=12 * MIB),
    )(own_piece, own_sides, inverse, paired, other, *pieces, *tips)


def tail_kernel(half, depth, known, inverse_in, pivots_in, packed_noise, packed_inverse, before, lower, upper, partial, out, noise, inverse, pivots, packed, thin, *rest):
    del partial
    initial, middle, forward, own, sides, sides_middle, sems, out_sems = rest
    layers, groups, _, columns = pivots.shape
    count = 2 * half
    last, one, other = last_two(half)
    part = lower.shape[0] // depth
    lines = thin.shape[1]
    at_one, at_other = (pl.ds(2 + (strip - last) * depth, depth) for strip in (one, other))
    copies = [
        pltpu.make_async_copy(strip_of(upper, layers - part, depth), noise.at[pl.ds(part, layers - part), at_one], sems.at[0]),
        pltpu.make_async_copy(strip_of(lower, part, depth), noise.at[pl.ds(0, part), at_one], sems.at[1]),
        pltpu.make_async_copy(strip_of(before, layers, depth), noise.at[:, at_other], sems.at[2]),
        pltpu.make_async_copy(known.at[:, pl.ds(0, 2)], noise.at[:, pl.ds(0, 2)], sems.at[3]),
        pltpu.make_async_copy(known.at[:, pl.ds(2, 2)], noise.at[:, pl.ds(2 * depth + 2, 2)], sems.at[4]),
        pltpu.make_async_copy(inverse_in, inverse, sems.at[6]),
        pltpu.make_async_copy(upper.at[pl.ds((layers - part) * depth, lines)], thin.at[0], sems.at[7]),
        pltpu.make_async_copy(before.at[pl.ds(layers * depth, lines)], thin.at[1], sems.at[8]),
    ]
    pivot_copy = pltpu.make_async_copy(pivots_in, pivots, sems.at[5])
    for copy in (*copies, pivot_copy):
        copy.start()
    inner = pl.ds(pl.multiple_of(last * depth * GROUP, GROUP), (groups + 2) * GROUP)
    packed[...] = packed_noise[inner, :]
    for copy in copies:
        copy.wait()
    for index, strip in enumerate((one, other)):
        unfold_into(packed, (2 + (strip - last) * depth) * GROUP, thin.at[index], depth * GROUP)

    def place_out(layer):
        return pltpu.make_async_copy(
            forward.at[layer + 1, pl.ds(1, 2 * depth)], out.at[layer, pl.ds(last * depth, 2 * depth)], out_sems.at[layer]
        )

    solve(
        noise, inverse, pivots, 0, packed[...], packed_inverse[inner, :],
        initial, middle, forward, (own, sides, sides_middle), pivot_copy.wait, lambda layer: place_out(layer).start(), layers,
    )

    def edge(own_group, to, sem):
        return pltpu.make_async_copy(forward.at[pl.ds(1, layers), pl.ds(own_group, 1)], out.at[:, pl.ds(to, 1)], sem)

    above = edge(0, jnp.maximum(last * depth - 1, 0), sems.at[0])
    below = edge(groups - 1, jnp.minimum((last + 2) * depth, count * depth - 1), sems.at[1])
    pl.when(last > 0)(above.start)
    pl.when(last < count - 2)(below.start)
    for layer in range(layers):
        place_out(layer).wait()
    pl.when(last > 0)(above.wait)
    pl.when(last < count - 2)(below.wait)


def solve_tail(sides, inverse, pivots, packed_noise, packed_inverse, before, lower, upper, partial, half, depth):
    layers, groups, _, columns = pivots.shape
    block = functools.partial(pltpu.VMEM, dtype=jnp.float32)
    return pl.pallas_call(
        functools.partial(tail_kernel, half, depth),
        in_specs=[ANYWHERE] * 3 + [WHOLE] * 2 + [ANYWHERE] * 4,
        out_specs=ANYWHERE,
        out_shape=f32(*partial.shape),
        scratch_shapes=[
            block((layers, groups + 2, GROUP, columns)),
            block((layers, groups + 2, GROUP, columns)),
            block((layers, groups, GROUP, columns)),
            block(((groups + 2) * GROUP, LANES)),
            block((2, before.shape[0] - layers * depth, GROUP, columns)),
            *solve_scratch(layers, groups, columns),
            pltpu.SemaphoreType.DMA((9,)),
            pltpu.SemaphoreType.DMA((layers,)),
        ],
        input_output_aliases={8: 0},
        compiler_params=pltpu.CompilerParams(vmem_limit_bytes=20 * MIB),
    )(sides, inverse, pivots, packed_noise, packed_inverse, before, lower, upper, partial)


def after(cells, *tokens):
    return lax.optimization_barrier((cells, *tokens))[0]


def body(noise, kappa, mask):
    layers, rows, width = noise.shape
    count = lax.axis_size("ay")
    across = lax.axis_size("ax")
    half = count // 2
    depth = rows // GROUP

    def swap(cells, step):
        return lax.ppermute(cells, "ay", [(i, i ^ step) for i in range(count)])

    def grouped(cells):
        return cells.reshape(layers, -1, GROUP, cells.shape[2])

    noise = grouped(noise)
    part = layers // 2
    first, own, split = count - 1, 0, half
    specs = {first: (first, 0, layers, True)}
    for step in [*range(count - 2, half, -1), *range(half - 1, 0, -1)]:
        specs[step] = (step, 0, layers, True)
    specs["lower"], specs["upper"] = (split, 0, part, False), (split, part, layers - part, True)
    specs[own] = (own, 0, 0, True)
    parts = {first: messages(noise, (specs.pop(first),), count)[0]}
    late = (half, half + 1)
    *made, tip = messages(after(noise, parts[first]), tuple(specs.values()), count, late)
    parts.update(zip(specs, made))
    inverse, pivots, packed = coefficients(after(kappa, parts[first]), mask)

    got = {first: swap(parts[first], first)}
    between = [pair for i in range(1, count - 1, 2) for pair in ((i, i + 1), (i + 1, i))]
    tip = lax.ppermute(tip, "ay", [(0, half), (count - 1, half - 1)])
    handed = swap(tip[tip.shape[0] // 2 :], 1)
    paired = swap(packed, 1)
    other = lax.ppermute(packed, "ay", between)
    for step in range(count - 2, half + 1, -1):
        got[step] = swap(after(parts[step], paired), step)
    got[half + 1] = swap(after(parts[half + 1], other, handed), half + 1)
    for step in range(half - 1, 1, -1):
        got[step] = swap(after(parts[step], other, handed), step)
    got[1] = swap(after(parts[1], got[first]), 1)
    lower = swap(after(parts["lower"], got[half + 2]), split)
    upper = swap(after(parts["upper"], got[half + 2]), split)
    inverse, pivots = grouped(inverse), grouped(pivots)

    steps = (0, *(step for step in range(count - 1, 0, -1) if step not in late))
    up, down = edges(
        noise, parts[0], inverse, paired, other, steps, [got[step] for step in steps[1:]], (tip, handed), count
    )
    above = lax.ppermute(down, "ax", [(i, i + 1) for i in range(across - 1)])
    below = lax.ppermute(up, "ax", [(i + 1, i) for i in range(across - 1)])
    partial, noise_part, inverse_part, pivots_part, packed_noise, packed_inverse = solve_block(
        inverse, pivots, noise, parts[0], [got[step] for step in steps[1:]], paired, other, above, below, half, depth
    )
    sample = solve_tail(
        noise_part, inverse_part, pivots_part, packed_noise, packed_inverse, got[half + 1], lower, upper, partial, half, depth
    )
    return sample.reshape(layers, rows * count, -1)


def solution(mesh):
    in_specs = (P(None, ("ax", "ay"), None), P(None, "ax", "ay"), P("ax", "ay"))
    out_specs = P(None, "ax", "ay")
    return jax.shard_map(body, mesh=mesh, in_specs=in_specs, out_specs=out_specs, check_vma=False)
```

time: 418 us -> 106 us (0.25)
  blocking collectives: 250 us -> 0 us
  local copies, waits for them, and re-layouts: 91.4 us -> 6.32 us
  other arithmetic: 63.9 us -> 0 us
  starting transfers between devices: 10.1 us -> 49.2 us
  waiting for transfers between devices: 0.63 us -> 26 us
  Pallas kernels: 0 us -> 24.1 us
    all_to_all x2 -> x0, blocking collectives: 250 us -> none  [the longest x1 145 us: body(): lax.all_to_all(stacked, 'ay', split_axis=1, concat_axis=2, tiled=True)]
    ppermute x4 -> x14, starting transfers between devices: 10.1 us -> 49.2 us  [the longest x10 40.1 us: swap(): return lax.ppermute(cells, 'ay', [(i, i ^ step) for i in range(count)])]
    unnamed x37 -> x10, local copies, waits for them, and re-layouts: 38.8 us -> 6.31 us
    ppermute x4 -> x14, waiting for transfers between devices: 0.63 us -> 26 us  [the longest x10 18.4 us: swap(): return lax.ppermute(cells, 'ay', [(i, i ^ step) for i in range(count)])]
    pallas_call x0 -> x6, Pallas kernels: none -> 24.1 us  [the longest x1 14.2 us: solve_block(): pl.pallas_call(functools.partial(block_kernel, half, depth), in_specs=[AN...]
    add x16 -> x0, local copies, waits for them, and re-layouts: 21.2 us -> none  [the longest x15 16.2 us: factors(): diagonal = 2.5 + kappa[layer_index]]
    mul x3 -> x0, other arithmetic: 19.3 us -> none  [the longest x2 15 us: body(): field = inverse * (noise + neighbours(padded))]
    unnamed x8 -> x0, other arithmetic: 17.2 us -> none
  transfers between devices with their start and end apart: 4 -> 14, of which waited for: 1 -> 6; matrix products, arithmetic and copies ran while one was open for 5% -> 0% of each run, Pallas kernels for 0% -> 19%
where the time goes in v2:
time: 106 us
  starting transfers between devices  49.2 us (46%)
  waiting for transfers between devices  26 us (25%)
  Pallas kernels  24.1 us (23%)
  local copies, waits for them, and re-layouts  6.32 us (6%)
    ppermute x10, starting transfers between devices, swap(): return lax.ppermute(cells, 'ay', [(i, i ^ step) for i in range(count)])  40.1 us
    ppermute x10, waiting for transfers between devices, swap(): return lax.ppermute(cells, 'ay', [(i, i ^ step) for i in range(count)])  18.4 us
    pallas_call x1, Pallas kernels, solve_block(): pl.pallas_call(functools.partial(block_kernel, half, depth), in_specs=[AN...  14.2 us
    unnamed x10, local copies, waits for them, and re-layouts  6.31 us
    ppermute x1, waiting for transfers between devices, body(): below = lax.ppermute(up, 'ax', [(i + 1, i) for i in range(across - 1)])  4.95 us
    pallas_call x1, Pallas kernels, solve_tail(): pl.pallas_call(functools.partial(tail_kernel, half, depth), in_specs=[ANY...  4.08 us
    ppermute x1, starting transfers between devices, body(): tip = lax.ppermute(tip, 'ay', [(0, half), (count - 1, half - 1)])  3.77 us
    ppermute x1, starting transfers between devices, body(): above = lax.ppermute(down, 'ax', [(i, i + 1) for i in range(across - 1)])  3.4 us
  transfers between devices with their start and end apart: 14, of which 6 were waited for; matrix products, arithmetic and copies ran while one was open for 0% of the time, Pallas kernels for 19%

profile of v2, /device:TPU:0, one launch (start us, length us, event | category | flops | bytes accessed | tf_op | source)
XLA Modules:
  0.0 105.8 jit_solution(4528966576608561031)
XLA Ops:
  0.0 0.0 copy-start
  0.0 2.2 %copy-done = f32[16,32,2048]{2,1,0:T(8,128)S(1)} copy-done((f32[16,32,2048]{2,1,0:T(8,128)S(1)}, f32[16,32,2048]{2,1,0:T(8,128)}, u32[]{:S(2)}) %copy-start) | copy-done | bytes 4194328
  2.2 0.0 copy-start.4
  2.2 0.0 copy-start.1
  2.2 0.4 shard_map.37
  2.6 4.6 %collective-permute-start = (f32[65,8,256]{2,1,0:T(8,128)S(1)}, f32[65,8,256]{2,1,0:T(8,128)S(1)}, u32[]{:S(2)}, u32[]{:S(2)}) collective-permute-start(f32[65,8,256]{2,1,0:T(8,128)S(1)} %shard_map.37), channel_id=1, source_target_pairs={{0,7},{1,6},{2,5},{3,4},{4,3},{5,2},{6,1},{7,0},{8,15},{9,14},{10,... | collective-permute-start | bytes 1597448 | tf_op jit(solution)/shard_map/ppermute | solution.py:585
  7.1 0.0 copy-done.4
  7.1 0.0 copy-start.2
  7.1 2.2 %copy-done.2 = f32[16,256,256]{2,1,0:T(8,128)S(1)} copy-done((f32[16,256,256]{2,1,0:T(8,128)S(1)}, f32[16,256,256]{2,1,0:T(8,128)}, u32[]{:S(2)}) %copy-start.2) | copy-done | bytes 4194328
  9.3 2.4 %shard_map.38 = (f32[16,256,256]{2,1,0:T(8,128)S(1)}, f32[16,256,256]{2,1,0:T(8,128)S(1)}, f32[256,128]{1,0:T(8,128)S(1)}) custom-call(f32[16,256,256]{2,1,0:T(8,128)S(1)} %copy-done.2, s32[256,256]{1,0:T(8,128)S(1)} %copy-done.4), custom_call_target="tpu_custom_call" | custom-call | tf_op jit(solution)/shard_map/pallas_call | solution.py:170
  11.7 0.0 copy-start.3
  11.7 1.9 %copy-done.3 = f32[16,256,256]{2,1,0:T(8,128)} copy-done((f32[16,256,256]{2,1,0:T(8,128)}, f32[16,256,256]{2,1,0:T(8,128)S(1)}, u32[]{:S(2)}) %copy-start.3) | copy-done | bytes 4194328
  13.7 0.7 collective-permute-start.1
  14.3 0.7 collective-permute-start.3
  15.0 0.0 copy-done.1
  15.0 2.7 %shard_map.39 = (f32[65,8,256]{2,1,0:T(8,128)S(1)}, f32[65,8,256]{2,1,0:T(8,128)S(1)}, f32[65,8,256]{2,1,0:T(8,128)S(1)}, f32[65,8,256]{2,1,0:T(8,128)S(1)}, f32...) custom-call(f32[16,4,8,2048]{3,2,1,0:T(8,128)S(1)} %bitcast.6), custom_call_target="tpu_custom_call" | custom-call | tf_op jit(solution)/shard_map/pallas_call | solution.py:134
  17.7 3.8 %collective-permute-start.4 = (f32[80,256]{1,0:T(8,128)S(1)}, f32[80,256]{1,0:T(8,128)S(1)}, u32[]{:S(2)}, u32[]{:S(2)}) collective-permute-start(f32[80,256]{1,0:T(8,128)S(1)} %get-tuple-element.43), channel_id=1, source_target_pairs={{0,4},{7,3},{8,12},{15,11},{16,20},{23,19},{24,28},{31,27}} | collective-permute-start | bytes 245768 | tf_op jit(solution)/shard_map/ppermute | solution.py:606
  21.5 2.0 %collective-permute-done.4.refs_5_ = f32[80,256]{1,0:T(8,128)S(1)} collective-permute-done((f32[80,256]{1,0:T(8,128)S(1)}, f32[80,256]{1,0:T(8,128)S(1)}, u32[]{:S(2)}, u32[]{:S(2)}) %collective-permute-start.4) | collective-permute-done | bytes 81952 | tf_op jit(solution)/shard_map/ppermute | solution.py:606
  23.6 0.0 collective-permute-start.5
  23.6 0.0 collective-permute-done.1.paired.refs_9_
  23.6 1.3 %collective-permute-start.2 = (f32[65,8,256]{2,1,0:T(8,128)S(1)}, f32[65,8,256]{2,1,0:T(8,128)S(1)}, u32[]{:S(2)}, u32[]{:S(2)}) collective-permute-start(f32[65,8,256]{2,1,0:T(8,128)S(1)} %get-tuple-element.41), channel_id=1, source_target_pairs={{0,6},{1,7},{2,4},{3,5},{4,2},{5,3},{6,0},{7,1},{8,14},{9,15},{10,... | collective-permute-start | bytes 1597448 | tf_op jit(solution)/shard_map/ppermute | solution.py:585
  24.9 0.0 collective-permute-done.5.refs_6_
  24.9 0.0 collective-permute-done.3.other.refs_10_
  24.9 21.2 %collective-permute-start.6 = (f32[65,8,256]{2,1,0:T(8,128)S(1)}, f32[65,8,256]{2,1,0:T(8,128)S(1)}, u32[]{:S(2)}, u32[]{:S(2)}) collective-permute-start(f32[65,8,256]{2,1,0:T(8,128)S(1)} %get-tuple-element.44), channel_id=1, source_target_pairs={{0,3},{1,2},{2,1},{3,0},{4,7},{5,6},{6,5},{7,4},{8,11},{9,10},{10,... | collective-permute-start | bytes 1597448 | tf_op jit(solution)/shard_map/ppermute | solution.py:585
  46.1 0.0 collective-permute-start.7
  46.1 0.0 collective-permute-done.refs_0_.refs_4_
  46.1 0.1 collective-permute-start.8
  46.3 2.8 %collective-permute-start.11 = (f32[65,8,256]{2,1,0:T(8,128)S(1)}, f32[65,8,256]{2,1,0:T(8,128)S(1)}, u32[]{:S(2)}, u32[]{:S(2)}) collective-permute-start(f32[65,8,256]{2,1,0:T(8,128)S(1)} %get-tuple-element.57), channel_id=1, source_target_pairs={{0,5},{1,4},{2,7},{3,6},{4,1},{5,0},{6,3},{7,2},{8,13},{9,12},{10,... | collective-permute-start | bytes 1597448 | tf_op jit(solution)/shard_map/ppermute | solution.py:585
  49.1 0.0 collective-permute-done.2.refs_1_.refs_5_
  49.1 8.0 %collective-permute-start.13 = (f32[33,8,256]{2,1,0:T(8,128)S(1)}, f32[33,8,256]{2,1,0:T(8,128)S(1)}, u32[]{:S(2)}, u32[]{:S(2)}) collective-permute-start(f32[33,8,256]{2,1,0:T(8,128)S(1)} %get-tuple-element.61), channel_id=1, source_target_pairs={{0,4},{1,5},{2,6},{3,7},{4,0},{5,1},{6,2},{7,3},{8,12},{9,13},{10,... | collective-permute-start | bytes 811016 | tf_op jit(solution)/shard_map/ppermute | solution.py:585
  57.1 5.5 %collective-permute-done.6.refs_2_.refs_6_ = f32[65,8,256]{2,1,0:T(8,128)S(1)} collective-permute-done((f32[65,8,256]{2,1,0:T(8,128)S(1)}, f32[65,8,256]{2,1,0:T(8,128)S(1)}, u32[]{:S(2)}, u32[]{:S(2)}) %collective-permute-start.6) | collective-permute-done | bytes 532512 | tf_op jit(solution)/shard_map/ppermute | solution.py:585
  62.6 1.4 %collective-permute-start.12 = (f32[32,8,256]{2,1,0:T(8,128)S(1)}, f32[32,8,256]{2,1,0:T(8,128)S(1)}, u32[]{:S(2)}, u32[]{:S(2)}) collective-permute-start(f32[32,8,256]{2,1,0:T(8,128)S(1)} %get-tuple-element.59), channel_id=1, source_target_pairs={{0,4},{1,5},{2,6},{3,7},{4,0},{5,1},{6,2},{7,3},{8,12},{9,13},{10,... | collective-permute-start | bytes 786440 | tf_op jit(solution)/shard_map/ppermute | solution.py:585
  64.0 8.2 %collective-permute-done.7.refs_3_.refs_7_ = f32[65,8,256]{2,1,0:T(8,128)S(1)} collective-permute-done((f32[65,8,256]{2,1,0:T(8,128)S(1)}, f32[65,8,256]{2,1,0:T(8,128)S(1)}, u32[]{:S(2)}, u32[]{:S(2)}) %collective-permute-start.7) | collective-permute-done | bytes 532512 | tf_op jit(solution)/shard_map/ppermute | solution.py:585
  72.2 0.0 collective-permute-done.8.refs_4_.refs_8_
  72.2 0.3 shard_map.40
  72.5 3.4 %collective-permute-start.9 = (f32[72,256]{1,0:T(8,128)S(1)}, f32[72,256]{1,0:T(8,128)S(1)}, u32[]{:S(2)}, u32[]{:S(2)}) collective-permute-start(f32[72,256]{1,0:T(8,128)S(1)} %get-tuple-element.49), channel_id=1, source_target_pairs={{0,8},{8,16},{16,24},{1,9},{9,17},{17,25},{2,10},{10,18},{18,26},{... | collective-permute-start | bytes 221192 | tf_op jit(solution)/shard_map/ppermute | solution.py:624
  75.9 1.3 %collective-permute-start.10 = (f32[72,256]{1,0:T(8,128)S(1)}, f32[72,256]{1,0:T(8,128)S(1)}, u32[]{:S(2)}, u32[]{:S(2)}) collective-permute-start(f32[72,256]{1,0:T(8,128)S(1)} %get-tuple-element.50), channel_id=1, source_target_pairs={{8,0},{16,8},{24,16},{9,1},{17,9},{25,17},{10,2},{18,10},{26,18},{... | collective-permute-start | bytes 221192 | tf_op jit(solution)/shard_map/ppermute | solution.py:625
  77.2 0.7 collective-permute-done.9.refs_11_
  77.9 5.0 %collective-permute-done.10.refs_12_ = f32[72,256]{1,0:T(8,128)S(1)} collective-permute-done((f32[72,256]{1,0:T(8,128)S(1)}, f32[72,256]{1,0:T(8,128)S(1)}, u32[]{:S(2)}, u32[]{:S(2)}) %collective-permute-start.10) | collective-permute-done | bytes 73760 | tf_op jit(solution)/shard_map/ppermute | solution.py:625
  82.8 14.2 %shard_map.41 = (f32[16,32,8,256]{3,2,1,0:T(8,128)}, f32[16,4,8,256]{3,2,1,0:T(8,128)S(1)}, f32[16,12,8,256]{3,2,1,0:T(8,128)S(1)}, f32[16,10,8,256]{3,2,1,0:T(8...) custom-call(f32[16,32,8,256]{3,2,1,0:T(8,128)S(1)} %bitcast.9, f32[16,32,8,256]{3,2,1,0:T(8,128)} %bitcast.10, ...), custom_call_target="tpu_custom_call" | custom-call | tf_op jit(solution)/shard_map/pallas_call | solution.py:398
  97.0 0.0 collective-permute-done.11.before
  97.1 4.7 %collective-permute-done.12.lower = f32[32,8,256]{2,1,0:T(8,128)S(1)} collective-permute-done((f32[32,8,256]{2,1,0:T(8,128)S(1)}, f32[32,8,256]{2,1,0:T(8,128)S(1)}, u32[]{:S(2)}, u32[]{:S(2)}) %collective-permute-start.12) | collective-permute-done | bytes 262176 | tf_op jit(solution)/shard_map/ppermute | solution.py:585
  101.7 0.0 collective-permute-done.13.upper
  101.7 4.1 %shard_map.42 = f32[16,32,8,256]{3,2,1,0:T(8,128)} custom-call(f32[16,4,8,256]{3,2,1,0:T(8,128)S(1)} %get-tuple-element.51.known, f32[16,12,8,256]{3,2,1,0:T(8,128)S(1)} %get-tuple-element.52.inverse_in, f32[16,10,8,256]{3,2,1,0:T(8,128)S(1)} %get-tuple-element.53.pivots_in, ...), custom_call_target="tpu_custom_call", output_to_operand_aliasing={{}: (8, {})} | custom-call | tf_op jit(solution)/shard_map/pallas_call | solution.py:553
  (1 shorter events, 0.0 us)
Async XLA Ops:
  0.0 2.2 %copy-start = (f32[16,32,2048]{2,1,0:T(8,128)S(1)}, f32[16,32,2048]{2,1,0:T(8,128)}, u32[]{:S(2)}) copy-start(f32[16,32,2048]{2,1,0:T(8,128)} %param.3) | copy-start | bytes 12582916
  2.2 5.0 %copy-start.4 = (s32[256,256]{1,0:T(8,128)S(1)}, s32[256,256]{1,0:T(8,128)}, u32[]{:S(2)}) copy-start(s32[256,256]{1,0:T(8,128)} %mask.1) | copy-start | bytes 786436
  2.2 12.8 %copy-start.1 = (f32[16,32,2048]{2,1,0:T(8,128)S(1)}, f32[16,32,2048]{2,1,0:T(8,128)}, u32[]{:S(2)}) copy-start(f32[16,32,2048]{2,1,0:T(8,128)} %param.3) | copy-start | bytes 12582916
  2.6 43.6 %collective-permute-start = (f32[65,8,256]{2,1,0:T(8,128)S(1)}, f32[65,8,256]{2,1,0:T(8,128)S(1)}, u32[]{:S(2)}, u32[]{:S(2)}) collective-permute-start(f32[65,8,256]{2,1,0:T(8,128)S(1)} %shard_map.37), channel_id=1, source_target_pairs={{0,7},{1,6},{2,5},{3,4},{4,3},{5,2},{6,1},{7,0},{8,15},{9,14},{10,... | collective-permute-start | bytes 1597448 | tf_op jit(solution)/shard_map/ppermute | solution.py:585
  7.1 2.2 %copy-start.2 = (f32[16,256,256]{2,1,0:T(8,128)S(1)}, f32[16,256,256]{2,1,0:T(8,128)}, u32[]{:S(2)}) copy-start(f32[16,256,256]{2,1,0:T(8,128)} %kappa) | copy-start | bytes 12582916
  11.7 1.9 %copy-start.3 = (f32[16,256,256]{2,1,0:T(8,128)}, f32[16,256,256]{2,1,0:T(8,128)S(1)}, u32[]{:S(2)}) copy-start(f32[16,256,256]{2,1,0:T(8,128)S(1)} %get-tuple-element.36) | copy-start | bytes 12582916
  13.7 9.9 %collective-permute-start.1 = (f32[256,128]{1,0:T(8,128)S(1)}, f32[256,128]{1,0:T(8,128)S(1)}, u32[]{:S(2)}, u32[]{:S(2)}) collective-permute-start(f32[256,128]{1,0:T(8,128)S(1)} %get-tuple-element.40), channel_id=1, source_target_pairs={{0,1},{1,0},{2,3},{3,2},{4,5},{5,4},{6,7},{7,6},{8,9},{9,8},{10,11... | collective-permute-start | bytes 393224 | tf_op jit(solution)/shard_map/ppermute | solution.py:585
  14.3 10.6 %collective-permute-start.3 = (f32[256,128]{1,0:T(8,128)S(1)}, f32[256,128]{1,0:T(8,128)S(1)}, u32[]{:S(2)}, u32[]{:S(2)}) collective-permute-start(f32[256,128]{1,0:T(8,128)S(1)} %get-tuple-element.40), channel_id=1, source_target_pairs={{1,2},{2,1},{3,4},{4,3},{5,6},{6,5},{9,10},{10,9},{11,12},{12,11},... | collective-permute-start | bytes 393224 | tf_op jit(solution)/shard_map/ppermute | solution.py:609
  17.7 5.8 %collective-permute-start.4 = (f32[80,256]{1,0:T(8,128)S(1)}, f32[80,256]{1,0:T(8,128)S(1)}, u32[]{:S(2)}, u32[]{:S(2)}) collective-permute-start(f32[80,256]{1,0:T(8,128)S(1)} %get-tuple-element.43), channel_id=1, source_target_pairs={{0,4},{7,3},{8,12},{15,11},{16,20},{23,19},{24,28},{31,27}} | collective-permute-start | bytes 245768 | tf_op jit(solution)/shard_map/ppermute | solution.py:606
  23.6 1.3 %collective-permute-start.5 = (f32[40,256]{1,0:T(8,128)S(1)}, f32[40,256]{1,0:T(8,128)S(1)}, u32[]{:S(2)}, u32[]{:S(2)}) collective-permute-start(f32[40,256]{1,0:T(8,128)S(1)} %slice.4), channel_id=1, source_target_pairs={{0,1},{1,0},{2,3},{3,2},{4,5},{5,4},{6,7},{7,6},{8,9},{9,8},{10,11... | collective-permute-start | bytes 122888 | tf_op jit(solution)/shard_map/ppermute | solution.py:585
  23.6 25.5 %collective-permute-start.2 = (f32[65,8,256]{2,1,0:T(8,128)S(1)}, f32[65,8,256]{2,1,0:T(8,128)S(1)}, u32[]{:S(2)}, u32[]{:S(2)}) collective-permute-start(f32[65,8,256]{2,1,0:T(8,128)S(1)} %get-tuple-element.41), channel_id=1, source_target_pairs={{0,6},{1,7},{2,4},{3,5},{4,2},{5,3},{6,0},{7,1},{8,14},{9,15},{10,... | collective-permute-start | bytes 1597448 | tf_op jit(solution)/shard_map/ppermute | solution.py:585
  24.9 37.7 %collective-permute-start.6 = (f32[65,8,256]{2,1,0:T(8,128)S(1)}, f32[65,8,256]{2,1,0:T(8,128)S(1)}, u32[]{:S(2)}, u32[]{:S(2)}) collective-permute-start(f32[65,8,256]{2,1,0:T(8,128)S(1)} %get-tuple-element.44), channel_id=1, source_target_pairs={{0,3},{1,2},{2,1},{3,0},{4,7},{5,6},{6,5},{7,4},{8,11},{9,10},{10,... | collective-permute-start | bytes 1597448 | tf_op jit(solution)/shard_map/ppermute | solution.py:585
  46.1 26.0 %collective-permute-start.7 = (f32[65,8,256]{2,1,0:T(8,128)S(1)}, f32[65,8,256]{2,1,0:T(8,128)S(1)}, u32[]{:S(2)}, u32[]{:S(2)}) collective-permute-start(f32[65,8,256]{2,1,0:T(8,128)S(1)} %get-tuple-element.46), channel_id=1, source_target_pairs={{0,2},{1,3},{2,0},{3,1},{4,6},{5,7},{6,4},{7,5},{8,10},{9,11},{10,... | collective-permute-start | bytes 1597448 | tf_op jit(solution)/shard_map/ppermute | solution.py:585
  46.1 26.0 %collective-permute-start.8 = (f32[65,8,256]{2,1,0:T(8,128)S(1)}, f32[65,8,256]{2,1,0:T(8,128)S(1)}, u32[]{:S(2)}, u32[]{:S(2)}) collective-permute-start(f32[65,8,256]{2,1,0:T(8,128)S(1)} %get-tuple-element.48), channel_id=1, source_target_pairs={{0,1},{1,0},{2,3},{3,2},{4,5},{5,4},{6,7},{7,6},{8,9},{9,8},{10,11... | collective-permute-start | bytes 1597448 | tf_op jit(solution)/shard_map/ppermute | solution.py:585
  46.3 50.8 %collective-permute-start.11 = (f32[65,8,256]{2,1,0:T(8,128)S(1)}, f32[65,8,256]{2,1,0:T(8,128)S(1)}, u32[]{:S(2)}, u32[]{:S(2)}) collective-permute-start(f32[65,8,256]{2,1,0:T(8,128)S(1)} %get-tuple-element.57), channel_id=1, source_target_pairs={{0,5},{1,4},{2,7},{3,6},{4,1},{5,0},{6,3},{7,2},{8,13},{9,12},{10,... | collective-permute-start | bytes 1597448 | tf_op jit(solution)/shard_map/ppermute | solution.py:585
  49.1 52.7 %collective-permute-start.13 = (f32[33,8,256]{2,1,0:T(8,128)S(1)}, f32[33,8,256]{2,1,0:T(8,128)S(1)}, u32[]{:S(2)}, u32[]{:S(2)}) collective-permute-start(f32[33,8,256]{2,1,0:T(8,128)S(1)} %get-tuple-element.61), channel_id=1, source_target_pairs={{0,4},{1,5},{2,6},{3,7},{4,0},{5,1},{6,2},{7,3},{8,12},{9,13},{10,... | collective-permute-start | bytes 811016 | tf_op jit(solution)/shard_map/ppermute | solution.py:585
  62.6 39.1 %collective-permute-start.12 = (f32[32,8,256]{2,1,0:T(8,128)S(1)}, f32[32,8,256]{2,1,0:T(8,128)S(1)}, u32[]{:S(2)}, u32[]{:S(2)}) collective-permute-start(f32[32,8,256]{2,1,0:T(8,128)S(1)} %get-tuple-element.59), channel_id=1, source_target_pairs={{0,4},{1,5},{2,6},{3,7},{4,0},{5,1},{6,2},{7,3},{8,12},{9,13},{10,... | collective-permute-start | bytes 786440 | tf_op jit(solution)/shard_map/ppermute | solution.py:585
  72.5 5.4 %collective-permute-start.9 = (f32[72,256]{1,0:T(8,128)S(1)}, f32[72,256]{1,0:T(8,128)S(1)}, u32[]{:S(2)}, u32[]{:S(2)}) collective-permute-start(f32[72,256]{1,0:T(8,128)S(1)} %get-tuple-element.49), channel_id=1, source_target_pairs={{0,8},{8,16},{16,24},{1,9},{9,17},{17,25},{2,10},{10,18},{18,26},{... | collective-permute-start | bytes 221192 | tf_op jit(solution)/shard_map/ppermute | solution.py:624
  75.9 6.9 %collective-permute-start.10 = (f32[72,256]{1,0:T(8,128)S(1)}, f32[72,256]{1,0:T(8,128)S(1)}, u32[]{:S(2)}, u32[]{:S(2)}) collective-permute-start(f32[72,256]{1,0:T(8,128)S(1)} %get-tuple-element.50), channel_id=1, source_target_pairs={{8,0},{16,8},{24,16},{9,1},{17,9},{25,17},{10,2},{18,10},{26,18},{... | collective-permute-start | bytes 221192 | tf_op jit(solution)/shard_map/ppermute | solution.py:625

commit v3 on v2

--- a/solution.py
+++ b/solution.py
@@ -588,7 +588,7 @@
         return cells.reshape(layers, -1, GROUP, cells.shape[2])
 
     noise = grouped(noise)
-    part = layers // 2
+    part = layers // 4
     first, own, split = count - 1, 0, half
     specs = {first: (first, 0, layers, True)}
     for step in [*range(count - 2, half, -1), *range(half - 1, 0, -1)]:

time: 106 us -> 118 us (1.11)
  waiting for transfers between devices: 26 us -> 45 us
  starting transfers between devices: 49.2 us -> 41.5 us
    ppermute x10, waiting for transfers between devices: 18.4 us -> 29 us  [swap(): return lax.ppermute(cells, 'ay', [(i, i ^ step) for i in range(count)])]
    ppermute x1, waiting for transfers between devices: 2.04 us -> 10.3 us  [body(): tip = lax.ppermute(tip, 'ay', [(0, half), (count - 1, half - 1)])]
    ppermute x10, starting transfers between devices: 40.1 us -> 32.1 us  [swap(): return lax.ppermute(cells, 'ay', [(i, i ^ step) for i in range(count)])]
  transfers between devices with their start and end apart: 14 -> 14, of which waited for: 6 -> 6; matrix products, arithmetic and copies ran while one was open for 0% -> 0% of each run, Pallas kernels for 19% -> 17%
where the time goes in v3:
time: 118 us; the launch traced here: 117 us
  waiting for transfers between devices  45 us (38%)
  starting transfers between devices  41.5 us (35%)
  Pallas kernels  24.1 us (20%)
  local copies, waits for them, and re-layouts  6.32 us (5%)
    ppermute x10, starting transfers between devices, swap(): return lax.ppermute(cells, 'ay', [(i, i ^ step) for i in range(count)])  32.1 us
    ppermute x10, waiting for transfers between devices, swap(): return lax.ppermute(cells, 'ay', [(i, i ^ step) for i in range(count)])  29 us
    pallas_call x1, Pallas kernels, solve_block(): pl.pallas_call(functools.partial(block_kernel, half, depth), in_specs=[AN...  14.2 us
    ppermute x1, waiting for transfers between devices, body(): tip = lax.ppermute(tip, 'ay', [(0, half), (count - 1, half - 1)])  10.3 us
    unnamed x10, local copies, waits for them, and re-layouts  6.31 us
    ppermute x1, waiting for transfers between devices, body(): below = lax.ppermute(up, 'ax', [(i + 1, i) for i in range(across - 1)])  5.05 us
    pallas_call x1, Pallas kernels, solve_tail(): pl.pallas_call(functools.partial(tail_kernel, half, depth), in_specs=[ANY...  4.13 us
    ppermute x1, starting transfers between devices, body(): tip = lax.ppermute(tip, 'ay', [(0, half), (count - 1, half - 1)])  3.99 us
  transfers between devices with their start and end apart: 14, of which 6 were waited for; matrix products, arithmetic and copies ran while one was open for 0% of the time, Pallas kernels for 17%

profile of v3, /device:TPU:0, one launch (start us, length us, event | category | flops | bytes accessed | tf_op | source)
XLA Modules:
  0.0 117.1 jit_solution(14095678558535604579)
XLA Ops:
  0.0 0.0 copy-start
  0.0 2.2 %copy-done = f32[16,32,2048]{2,1,0:T(8,128)S(1)} copy-done((f32[16,32,2048]{2,1,0:T(8,128)S(1)}, f32[16,32,2048]{2,1,0:T(8,128)}, u32[]{:S(2)}) %copy-start) | copy-done | bytes 4194328
  2.2 0.0 copy-start.4
  2.2 0.0 copy-start.1
  2.2 0.4 shard_map.37
  2.6 4.6 %collective-permute-start = (f32[65,8,256]{2,1,0:T(8,128)S(1)}, f32[65,8,256]{2,1,0:T(8,128)S(1)}, u32[]{:S(2)}, u32[]{:S(2)}) collective-permute-start(f32[65,8,256]{2,1,0:T(8,128)S(1)} %shard_map.37), channel_id=1, source_target_pairs={{0,7},{1,6},{2,5},{3,4},{4,3},{5,2},{6,1},{7,0},{8,15},{9,14},{10,... | collective-permute-start | bytes 1597448 | tf_op jit(solution)/shard_map/ppermute | solution.py:585
  7.1 0.0 copy-done.4
  7.1 0.0 copy-start.2
  7.1 2.2 %copy-done.2 = f32[16,256,256]{2,1,0:T(8,128)S(1)} copy-done((f32[16,256,256]{2,1,0:T(8,128)S(1)}, f32[16,256,256]{2,1,0:T(8,128)}, u32[]{:S(2)}) %copy-start.2) | copy-done | bytes 4194328
  9.3 2.4 %shard_map.38 = (f32[16,256,256]{2,1,0:T(8,128)S(1)}, f32[16,256,256]{2,1,0:T(8,128)S(1)}, f32[256,128]{1,0:T(8,128)S(1)}) custom-call(f32[16,256,256]{2,1,0:T(8,128)S(1)} %copy-done.2, s32[256,256]{1,0:T(8,128)S(1)} %copy-done.4), custom_call_target="tpu_custom_call" | custom-call | tf_op jit(solution)/shard_map/pallas_call | solution.py:170
  11.7 0.0 copy-start.3
  11.7 1.9 %copy-done.3 = f32[16,256,256]{2,1,0:T(8,128)} copy-done((f32[16,256,256]{2,1,0:T(8,128)}, f32[16,256,256]{2,1,0:T(8,128)S(1)}, u32[]{:S(2)}) %copy-start.3) | copy-done | bytes 4194328
  13.7 0.7 collective-permute-start.1
  14.3 0.0 copy-done.1
  14.3 2.7 %shard_map.39 = (f32[65,8,256]{2,1,0:T(8,128)S(1)}, f32[65,8,256]{2,1,0:T(8,128)S(1)}, f32[65,8,256]{2,1,0:T(8,128)S(1)}, f32[65,8,256]{2,1,0:T(8,128)S(1)}, f32...) custom-call(f32[16,4,8,2048]{3,2,1,0:T(8,128)S(1)} %bitcast.6), custom_call_target="tpu_custom_call" | custom-call | tf_op jit(solution)/shard_map/pallas_call | solution.py:134
  17.1 0.0 collective-permute-done.1.paired.refs_9_
  17.1 0.8 collective-permute-start.2
  17.9 0.7 collective-permute-start.3
  18.6 4.0 %collective-permute-start.4 = (f32[80,256]{1,0:T(8,128)S(1)}, f32[80,256]{1,0:T(8,128)S(1)}, u32[]{:S(2)}, u32[]{:S(2)}) collective-permute-start(f32[80,256]{1,0:T(8,128)S(1)} %get-tuple-element.43), channel_id=1, source_target_pairs={{0,4},{7,3},{8,12},{15,11},{16,20},{23,19},{24,28},{31,27}} | collective-permute-start | bytes 245768 | tf_op jit(solution)/shard_map/ppermute | solution.py:606
  22.6 10.3 %collective-permute-done.4.refs_5_ = f32[80,256]{1,0:T(8,128)S(1)} collective-permute-done((f32[80,256]{1,0:T(8,128)S(1)}, f32[80,256]{1,0:T(8,128)S(1)}, u32[]{:S(2)}, u32[]{:S(2)}) %collective-permute-start.4) | collective-permute-done | bytes 81952 | tf_op jit(solution)/shard_map/ppermute | solution.py:606
  32.9 0.0 collective-permute-start.5
  32.9 1.2 %collective-permute-done.5.refs_6_ = f32[40,256]{1,0:T(8,128)S(1)} collective-permute-done((f32[40,256]{1,0:T(8,128)S(1)}, f32[40,256]{1,0:T(8,128)S(1)}, u32[]{:S(2)}, u32[]{:S(2)}) %collective-permute-start.5) | collective-permute-done | bytes 40992 | tf_op jit(solution)/shard_map/ppermute | solution.py:585
  34.1 0.0 collective-permute-done.3.other.refs_10_
  34.1 21.9 %collective-permute-start.6 = (f32[65,8,256]{2,1,0:T(8,128)S(1)}, f32[65,8,256]{2,1,0:T(8,128)S(1)}, u32[]{:S(2)}, u32[]{:S(2)}) collective-permute-start(f32[65,8,256]{2,1,0:T(8,128)S(1)} %get-tuple-element.44), channel_id=1, source_target_pairs={{0,3},{1,2},{2,1},{3,0},{4,7},{5,6},{6,5},{7,4},{8,11},{9,10},{10,... | collective-permute-start | bytes 1597448 | tf_op jit(solution)/shard_map/ppermute | solution.py:585
  56.0 0.0 collective-permute-start.7
  56.0 0.0 collective-permute-done.refs_0_.refs_4_
  56.0 0.1 collective-permute-start.8
  56.2 2.9 %collective-permute-start.11 = (f32[65,8,256]{2,1,0:T(8,128)S(1)}, f32[65,8,256]{2,1,0:T(8,128)S(1)}, u32[]{:S(2)}, u32[]{:S(2)}) collective-permute-start(f32[65,8,256]{2,1,0:T(8,128)S(1)} %get-tuple-element.57), channel_id=1, source_target_pairs={{0,5},{1,4},{2,7},{3,6},{4,1},{5,0},{6,3},{7,2},{8,13},{9,12},{10,... | collective-permute-start | bytes 1597448 | tf_op jit(solution)/shard_map/ppermute | solution.py:585
  59.1 0.0 collective-permute-done.2.refs_1_.refs_5_
  59.1 0.4 collective-permute-start.13
  59.5 23.7 %collective-permute-done.6.refs_2_.refs_6_ = f32[65,8,256]{2,1,0:T(8,128)S(1)} collective-permute-done((f32[65,8,256]{2,1,0:T(8,128)S(1)}, f32[65,8,256]{2,1,0:T(8,128)S(1)}, u32[]{:S(2)}, u32[]{:S(2)}) %collective-permute-start.6) | collective-permute-done | bytes 532512 | tf_op jit(solution)/shard_map/ppermute | solution.py:585
  83.2 0.7 collective-permute-start.12
  83.8 4.1 %collective-permute-done.7.refs_3_.refs_7_ = f32[65,8,256]{2,1,0:T(8,128)S(1)} collective-permute-done((f32[65,8,256]{2,1,0:T(8,128)S(1)}, f32[65,8,256]{2,1,0:T(8,128)S(1)}, u32[]{:S(2)}, u32[]{:S(2)}) %collective-permute-start.7) | collective-permute-done | bytes 532512 | tf_op jit(solution)/shard_map/ppermute | solution.py:585
  87.9 0.0 collective-permute-done.8.refs_4_.refs_8_
  87.9 0.3 shard_map.40
  88.3 3.4 %collective-permute-start.9 = (f32[72,256]{1,0:T(8,128)S(1)}, f32[72,256]{1,0:T(8,128)S(1)}, u32[]{:S(2)}, u32[]{:S(2)}) collective-permute-start(f32[72,256]{1,0:T(8,128)S(1)} %get-tuple-element.49), channel_id=1, source_target_pairs={{0,8},{8,16},{16,24},{1,9},{9,17},{17,25},{2,10},{10,18},{18,26},{... | collective-permute-start | bytes 221192 | tf_op jit(solution)/shard_map/ppermute | solution.py:624
  91.7 1.3 %collective-permute-start.10 = (f32[72,256]{1,0:T(8,128)S(1)}, f32[72,256]{1,0:T(8,128)S(1)}, u32[]{:S(2)}, u32[]{:S(2)}) collective-permute-start(f32[72,256]{1,0:T(8,128)S(1)} %get-tuple-element.50), channel_id=1, source_target_pairs={{8,0},{16,8},{24,16},{9,1},{17,9},{25,17},{10,2},{18,10},{26,18},{... | collective-permute-start | bytes 221192 | tf_op jit(solution)/shard_map/ppermute | solution.py:625
  93.0 0.7 collective-permute-done.9.refs_11_
  93.6 5.1 %collective-permute-done.10.refs_12_ = f32[72,256]{1,0:T(8,128)S(1)} collective-permute-done((f32[72,256]{1,0:T(8,128)S(1)}, f32[72,256]{1,0:T(8,128)S(1)}, u32[]{:S(2)}, u32[]{:S(2)}) %collective-permute-start.10) | collective-permute-done | bytes 73760 | tf_op jit(solution)/shard_map/ppermute | solution.py:625
  98.7 14.2 %shard_map.41 = (f32[16,32,8,256]{3,2,1,0:T(8,128)}, f32[16,4,8,256]{3,2,1,0:T(8,128)S(1)}, f32[16,12,8,256]{3,2,1,0:T(8,128)S(1)}, f32[16,10,8,256]{3,2,1,0:T(8...) custom-call(f32[16,32,8,256]{3,2,1,0:T(8,128)S(1)} %bitcast.9, f32[16,32,8,256]{3,2,1,0:T(8,128)} %bitcast.10, ...), custom_call_target="tpu_custom_call" | custom-call | tf_op jit(solution)/shard_map/pallas_call | solution.py:398
  112.9 0.0 collective-permute-done.11.before
  112.9 0.0 collective-permute-done.12.lower
  112.9 0.0 collective-permute-done.13.upper
  112.9 4.1 %shard_map.42 = f32[16,32,8,256]{3,2,1,0:T(8,128)} custom-call(f32[16,4,8,256]{3,2,1,0:T(8,128)S(1)} %get-tuple-element.51.known, f32[16,12,8,256]{3,2,1,0:T(8,128)S(1)} %get-tuple-element.52.inverse_in, f32[16,10,8,256]{3,2,1,0:T(8,128)S(1)} %get-tuple-element.53.pivots_in, ...), custom_call_target="tpu_custom_call", output_to_operand_aliasing={{}: (8, {})} | custom-call | tf_op jit(solution)/shard_map/pallas_call | solution.py:553
  (1 shorter events, 0.0 us)
Async XLA Ops:
  0.0 2.2 %copy-start = (f32[16,32,2048]{2,1,0:T(8,128)S(1)}, f32[16,32,2048]{2,1,0:T(8,128)}, u32[]{:S(2)}) copy-start(f32[16,32,2048]{2,1,0:T(8,128)} %param.3) | copy-start | bytes 12582916
  2.2 5.0 %copy-start.4 = (s32[256,256]{1,0:T(8,128)S(1)}, s32[256,256]{1,0:T(8,128)}, u32[]{:S(2)}) copy-start(s32[256,256]{1,0:T(8,128)} %mask.1) | copy-start | bytes 786436
  2.2 12.2 %copy-start.1 = (f32[16,32,2048]{2,1,0:T(8,128)S(1)}, f32[16,32,2048]{2,1,0:T(8,128)}, u32[]{:S(2)}) copy-start(f32[16,32,2048]{2,1,0:T(8,128)} %param.3) | copy-start | bytes 12582916
  2.6 53.4 %collective-permute-start = (f32[65,8,256]{2,1,0:T(8,128)S(1)}, f32[65,8,256]{2,1,0:T(8,128)S(1)}, u32[]{:S(2)}, u32[]{:S(2)}) collective-permute-start(f32[65,8,256]{2,1,0:T(8,128)S(1)} %shard_map.37), channel_id=1, source_target_pairs={{0,7},{1,6},{2,5},{3,4},{4,3},{5,2},{6,1},{7,0},{8,15},{9,14},{10,... | collective-permute-start | bytes 1597448 | tf_op jit(solution)/shard_map/ppermute | solution.py:585
  7.1 2.2 %copy-start.2 = (f32[16,256,256]{2,1,0:T(8,128)S(1)}, f32[16,256,256]{2,1,0:T(8,128)}, u32[]{:S(2)}) copy-start(f32[16,256,256]{2,1,0:T(8,128)} %kappa) | copy-start | bytes 12582916
  11.7 1.9 %copy-start.3 = (f32[16,256,256]{2,1,0:T(8,128)}, f32[16,256,256]{2,1,0:T(8,128)S(1)}, u32[]{:S(2)}) copy-start(f32[16,256,256]{2,1,0:T(8,128)S(1)} %get-tuple-element.36) | copy-start | bytes 12582916
  13.7 3.4 %collective-permute-start.1 = (f32[256,128]{1,0:T(8,128)S(1)}, f32[256,128]{1,0:T(8,128)S(1)}, u32[]{:S(2)}, u32[]{:S(2)}) collective-permute-start(f32[256,128]{1,0:T(8,128)S(1)} %get-tuple-element.40), channel_id=1, source_target_pairs={{0,1},{1,0},{2,3},{3,2},{4,5},{5,4},{6,7},{7,6},{8,9},{9,8},{10,11... | collective-permute-start | bytes 393224 | tf_op jit(solution)/shard_map/ppermute | solution.py:585
  17.1 42.0 %collective-permute-start.2 = (f32[65,8,256]{2,1,0:T(8,128)S(1)}, f32[65,8,256]{2,1,0:T(8,128)S(1)}, u32[]{:S(2)}, u32[]{:S(2)}) collective-permute-start(f32[65,8,256]{2,1,0:T(8,128)S(1)} %get-tuple-element.41), channel_id=1, source_target_pairs={{0,6},{1,7},{2,4},{3,5},{4,2},{5,3},{6,0},{7,1},{8,14},{9,15},{10,... | collective-permute-start | bytes 1597448 | tf_op jit(solution)/shard_map/ppermute | solution.py:585
  17.9 16.2 %collective-permute-start.3 = (f32[256,128]{1,0:T(8,128)S(1)}, f32[256,128]{1,0:T(8,128)S(1)}, u32[]{:S(2)}, u32[]{:S(2)}) collective-permute-start(f32[256,128]{1,0:T(8,128)S(1)} %get-tuple-element.40), channel_id=1, source_target_pairs={{1,2},{2,1},{3,4},{4,3},{5,6},{6,5},{9,10},{10,9},{11,12},{12,11},... | collective-permute-start | bytes 393224 | tf_op jit(solution)/shard_map/ppermute | solution.py:609
  18.6 14.3 %collective-permute-start.4 = (f32[80,256]{1,0:T(8,128)S(1)}, f32[80,256]{1,0:T(8,128)S(1)}, u32[]{:S(2)}, u32[]{:S(2)}) collective-permute-start(f32[80,256]{1,0:T(8,128)S(1)} %get-tuple-element.43), channel_id=1, source_target_pairs={{0,4},{7,3},{8,12},{15,11},{16,20},{23,19},{24,28},{31,27}} | collective-permute-start | bytes 245768 | tf_op jit(solution)/shard_map/ppermute | solution.py:606
  32.9 1.2 %collective-permute-start.5 = (f32[40,256]{1,0:T(8,128)S(1)}, f32[40,256]{1,0:T(8,128)S(1)}, u32[]{:S(2)}, u32[]{:S(2)}) collective-permute-start(f32[40,256]{1,0:T(8,128)S(1)} %slice.4), channel_id=1, source_target_pairs={{0,1},{1,0},{2,3},{3,2},{4,5},{5,4},{6,7},{7,6},{8,9},{9,8},{10,11... | collective-permute-start | bytes 122888 | tf_op jit(solution)/shard_map/ppermute | solution.py:585
  34.1 49.1 %collective-permute-start.6 = (f32[65,8,256]{2,1,0:T(8,128)S(1)}, f32[65,8,256]{2,1,0:T(8,128)S(1)}, u32[]{:S(2)}, u32[]{:S(2)}) collective-permute-start(f32[65,8,256]{2,1,0:T(8,128)S(1)} %get-tuple-element.44), channel_id=1, source_target_pairs={{0,3},{1,2},{2,1},{3,0},{4,7},{5,6},{6,5},{7,4},{8,11},{9,10},{10,... | collective-permute-start | bytes 1597448 | tf_op jit(solution)/shard_map/ppermute | solution.py:585
  56.0 31.9 %collective-permute-start.7 = (f32[65,8,256]{2,1,0:T(8,128)S(1)}, f32[65,8,256]{2,1,0:T(8,128)S(1)}, u32[]{:S(2)}, u32[]{:S(2)}) collective-permute-start(f32[65,8,256]{2,1,0:T(8,128)S(1)} %get-tuple-element.46), channel_id=1, source_target_pairs={{0,2},{1,3},{2,0},{3,1},{4,6},{5,7},{6,4},{7,5},{8,10},{9,11},{10,... | collective-permute-start | bytes 1597448 | tf_op jit(solution)/shard_map/ppermute | solution.py:585
  56.0 31.9 %collective-permute-start.8 = (f32[65,8,256]{2,1,0:T(8,128)S(1)}, f32[65,8,256]{2,1,0:T(8,128)S(1)}, u32[]{:S(2)}, u32[]{:S(2)}) collective-permute-start(f32[65,8,256]{2,1,0:T(8,128)S(1)} %get-tuple-element.48), channel_id=1, source_target_pairs={{0,1},{1,0},{2,3},{3,2},{4,5},{5,4},{6,7},{7,6},{8,9},{9,8},{10,11... | collective-permute-start | bytes 1597448 | tf_op jit(solution)/shard_map/ppermute | solution.py:585
  56.2 56.7 %collective-permute-start.11 = (f32[65,8,256]{2,1,0:T(8,128)S(1)}, f32[65,8,256]{2,1,0:T(8,128)S(1)}, u32[]{:S(2)}, u32[]{:S(2)}) collective-permute-start(f32[65,8,256]{2,1,0:T(8,128)S(1)} %get-tuple-element.57), channel_id=1, source_target_pairs={{0,5},{1,4},{2,7},{3,6},{4,1},{5,0},{6,3},{7,2},{8,13},{9,12},{10,... | collective-permute-start | bytes 1597448 | tf_op jit(solution)/shard_map/ppermute | solution.py:585
  59.1 53.8 %collective-permute-start.13 = (f32[49,8,256]{2,1,0:T(8,128)S(1)}, f32[49,8,256]{2,1,0:T(8,128)S(1)}, u32[]{:S(2)}, u32[]{:S(2)}) collective-permute-start(f32[49,8,256]{2,1,0:T(8,128)S(1)} %get-tuple-element.61), channel_id=1, source_target_pairs={{0,4},{1,5},{2,6},{3,7},{4,0},{5,1},{6,2},{7,3},{8,12},{9,13},{10,... | collective-permute-start | bytes 1204232 | tf_op jit(solution)/shard_map/ppermute | solution.py:585
  83.2 29.8 %collective-permute-start.12 = (f32[16,8,256]{2,1,0:T(8,128)S(1)}, f32[16,8,256]{2,1,0:T(8,128)S(1)}, u32[]{:S(2)}, u32[]{:S(2)}) collective-permute-start(f32[16,8,256]{2,1,0:T(8,128)S(1)} %get-tuple-element.59), channel_id=1, source_target_pairs={{0,4},{1,5},{2,6},{3,7},{4,0},{5,1},{6,2},{7,3},{8,12},{9,13},{10,... | collective-permute-start | bytes 393224 | tf_op jit(solution)/shard_map/ppermute | solution.py:585
  88.3 5.4 %collective-permute-start.9 = (f32[72,256]{1,0:T(8,128)S(1)}, f32[72,256]{1,0:T(8,128)S(1)}, u32[]{:S(2)}, u32[]{:S(2)}) collective-permute-start(f32[72,256]{1,0:T(8,128)S(1)} %get-tuple-element.49), channel_id=1, source_target_pairs={{0,8},{8,16},{16,24},{1,9},{9,17},{17,25},{2,10},{10,18},{18,26},{... | collective-permute-start | bytes 221192 | tf_op jit(solution)/shard_map/ppermute | solution.py:624
  91.7 7.0 %collective-permute-start.10 = (f32[72,256]{1,0:T(8,128)S(1)}, f32[72,256]{1,0:T(8,128)S(1)}, u32[]{:S(2)}, u32[]{:S(2)}) collective-permute-start(f32[72,256]{1,0:T(8,128)S(1)} %get-tuple-element.50), channel_id=1, source_target_pairs={{8,0},{16,8},{24,16},{9,1},{17,9},{25,17},{10,2},{18,10},{26,18},{... | collective-permute-start | bytes 221192 | tf_op jit(solution)/shard_map/ppermute | solution.py:625
